TPU v7x, 256 devices: a whole 4x4x8 slice. The times are simulated.
256 devices in a mesh: grp: 8 (over y, core), wide: 32 (over z, x).
Axes of the slice: x: 4, y: 4, z: 8, core: 2. Of those that a mesh axis runs over, the one named last changes fastest.
Arguments:
- features: bfloat16 [2048, 128, 128], P(('grp', 'wide')), may hold values from -6 to 6
- group_src: int32 [2048, 8], P(('grp', 'wide')), may hold values from 0 to 63
- group_count: int32 [2048], P(('grp', 'wide')), may hold values from 1 to 8
- group_tiles: bfloat16 [2048, 8, 128, 128], P(('grp', 'wide')), may hold values from 0 to 2, as said below
- hist_owner: int32 [2048, 4, 1], P(('grp', 'wide')), may hold values from 0 to 31; in each aligned block of 32 rows (0 to 31, 32 to 63, ..., all dimensions but the last counted through in order) at most 2 rows name the same one
- hist_local: int32 [2048, 4], P(('grp', 'wide')), may hold values from 0 to 3
- hist_count: int32 [2048], P(('grp', 'wide')), may hold values from 1 to 4
- hist_tiles: bfloat16 [2048, 4, 128, 128], P(('grp', 'wide')), may hold values from 0 to 2, as said below
- feature_store: bfloat16 [128, 128, 128], P('wide'), may hold values from -6 to 6
- hidden_store: bfloat16 [128, 128, 256], P('wide'), may hold values from -4 to 4
- self_one: bfloat16 [128, 256], replicated, may hold values from -0.5 to 0.5
- neigh_one: bfloat16 [128, 256], replicated, may hold values from -2 to 2
- self_two: bfloat16 [256, 256], replicated, may hold values from -0.375 to 0.375
- neigh_two: bfloat16 [256, 256], replicated, may hold values from -1.5 to 1.5
- cotangent: bfloat16 [2048, 128, 256], P(('grp', 'wide')), may hold values from -0.01171875 to 0.01171875
Outputs:
- embedding: bfloat16 [2048, 128, 256], P(('grp', 'wide'))
- grad_self_one: float32 [128, 256], replicated
- grad_neigh_one: float32 [128, 256], replicated
- grad_self_two: float32 [256, 256], replicated
- grad_neigh_two: float32 [256, 256], replicated
Inputs may be any that keep to these rules, and one draw needn't show every extreme that they name: `group_src`: index of a cluster within the group of the slot's batch cluster. `hist_owner`: among the 8 x 4 history slots of one device, no owner is named more than 2 times. `group_tiles`: nonnegative edge weights. `hist_tiles`: nonnegative edge weights.
All inputs are finite; a program needn't handle non-finite values.
Results may differ from a plain program's by a relative error of at most 0.009.
Values may be sent and summed in bfloat16 or wider, within the bound.
A program may use at most 128 MiB of HBM per device.

v0:
```python
import jax
import jax.numpy as jnp
from jax import lax
from jax.sharding import PartitionSpec as P


def aggregate(tiles_near, blocks_near, tiles_far, blocks_far):
    inside = jnp.einsum(
        "csrj,csjf->crf", tiles_near, blocks_near, preferred_element_type=jnp.float32
    )
    outside = jnp.einsum(
        "csrj,csjf->crf", tiles_far, blocks_far, preferred_element_type=jnp.float32
    )
    return inside + outside


def body(
    features,
    group_src,
    group_count,
    group_tiles,
    hist_owner,
    hist_local,
    hist_count,
    hist_tiles,
    feature_store,
    hidden_store,
    self_one,
    neigh_one,
    self_two,
    neigh_two,
    cotangent,
):
    clusters, block, width_in = features.shape
    slots_near = group_src.shape[1]
    slots_far = hist_local.shape[1]
    width_hid = self_one.shape[1]
    live_near = (jnp.arange(slots_near)[None, :] < group_count[:, None]).astype(jnp.bfloat16)
    live_far = (jnp.arange(slots_far)[None, :] < hist_count[:, None]).astype(jnp.bfloat16)
    tiles_near = group_tiles * live_near[:, :, None, None]
    tiles_far = hist_tiles * live_far[:, :, None, None]
    degree = (
        1.0
        + jnp.sum(tiles_near, axis=(1, 3), dtype=jnp.float32)
        + jnp.sum(tiles_far, axis=(1, 3), dtype=jnp.float32)
    )
    owners = hist_owner.reshape(-1)
    local_ids = hist_local.reshape(-1)
    whole_feat, whole_hid = (
        lax.all_gather(feature_store, "wide", axis=0, tiled=True),
        lax.all_gather(hidden_store, "wide", axis=0, tiled=True),
    )
    wanted = owners * feature_store.shape[0] + local_ids
    far_feat = jnp.take(whole_feat, wanted, axis=0)
    far_hid = jnp.take(whole_hid, wanted, axis=0)
    far_feat = far_feat.reshape(clusters, slots_far, block, width_in)
    far_hid = far_hid.reshape(clusters, slots_far, block, width_hid)
    sources = group_src.reshape(-1)
    group_feat = lax.all_gather(features, "grp", axis=0, tiled=True)
    near_feat = jnp.take(group_feat, sources, axis=0).reshape(clusters, slots_near, block, width_in)
    mean_one = (aggregate(tiles_near, near_feat, tiles_far, far_feat) / degree[:, :, None]).astype(
        jnp.bfloat16
    )
    flat = features.reshape(-1, width_in)
    mean_flat = mean_one.reshape(-1, width_in)
    pre_one = jnp.dot(flat, self_one, preferred_element_type=jnp.float32) + jnp.dot(
        mean_flat, neigh_one, preferred_element_type=jnp.float32
    )
    hidden = jax.nn.silu(pre_one).astype(jnp.bfloat16)
    group_hid = lax.all_gather(
        hidden.reshape(clusters, block, width_hid), "grp", axis=0, tiled=True
    )
    near_hid = jnp.take(group_hid, sources, axis=0).reshape(clusters, slots_near, block, width_hid)
    mean_two = (aggregate(tiles_near, near_hid, tiles_far, far_hid) / degree[:, :, None]).astype(
        jnp.bfloat16
    )
    mean_two_flat = mean_two.reshape(-1, width_hid)
    pre_two = jnp.dot(hidden, self_two, preferred_element_type=jnp.float32) + jnp.dot(
        mean_two_flat, neigh_two, preferred_element_type=jnp.float32
    )
    embedding = pre_two.astype(jnp.bfloat16).reshape(clusters, block, width_hid)
    upstream = cotangent.reshape(-1, width_hid)
    grad_self_two = jnp.einsum("nd,nf->df", hidden, upstream, preferred_element_type=jnp.float32)
    grad_neigh_two = jnp.einsum(
        "nd,nf->df", mean_two_flat, upstream, preferred_element_type=jnp.float32
    )
    through_neigh = jnp.einsum("nf,df->nd", upstream, neigh_two, preferred_element_type=jnp.float32)
    scaled = (through_neigh.reshape(clusters, block, width_hid) / degree[:, :, None]).astype(
        jnp.bfloat16
    )
    slot_terms = jnp.einsum(
        "csrj,crf->csjf", tiles_near, scaled, preferred_element_type=jnp.float32
    ).reshape(clusters * slots_near, block, width_hid)
    group_rows = group_feat.shape[0]
    by_target = jax.ops.segment_sum(slot_terms, sources, num_segments=group_rows)
    returned = lax.psum_scatter(
        by_target.astype(jnp.bfloat16), "grp", scatter_dimension=0, tiled=True
    ).astype(jnp.float32)
    through_self = jnp.einsum("nf,df->nd", upstream, self_two, preferred_element_type=jnp.float32)
    total = through_self + returned.reshape(-1, width_hid)
    sigma = jax.nn.sigmoid(pre_one)
    grad_pre = (total * sigma * (1.0 + pre_one * (1.0 - sigma))).astype(jnp.bfloat16)
    grad_self_one = jnp.einsum("nd,nf->df", flat, grad_pre, preferred_element_type=jnp.float32)
    grad_neigh_one = jnp.einsum(
        "nd,nf->df", mean_flat, grad_pre, preferred_element_type=jnp.float32
    )
    summed = lax.psum(
        (grad_self_one, grad_neigh_one, grad_self_two, grad_neigh_two), ("grp", "wide")
    )
    return (embedding, summed[0], summed[1], summed[2], summed[3])


def solution(mesh):
    placed = (
        P(("grp", "wide"), None, None),
        P(("grp", "wide"), None),
        P(("grp", "wide")),
        P(("grp", "wide"), None, None, None),
        P(("grp", "wide"), None, None),
        P(("grp", "wide"), None),
        P(("grp", "wide")),
        P(("grp", "wide"), None, None, None),
        P("wide", None, None),
        P("wide", None, None),
        P(),
        P(),
        P(),
        P(),
        P(("grp", "wide"), None, None),
    )
    return jax.shard_map(
        body,
        mesh=mesh,
        in_specs=placed,
        out_specs=(P(("grp", "wide"), None, None), P(), P(), P(), P()),
        check_vma=False,
    )
```

profile of v0, /device:TPU:1, one launch (start us, length us, event | category | flops | bytes accessed | tf_op | source)
XLA Modules:
  0.0 576.7 jit_solution(8877855241022781067)
XLA Ops:
  7.2 0.0 copy-start
  7.2 0.0 copy-start.1
  7.2 0.0 copy-start.7
  7.2 0.0 all-gather.5.cloned.1.call-start
  7.2 0.7 all-gather.5.cloned.1.call-update
  7.9 0.0 all-gather.7.cloned.1.call-start
  8.0 0.7 all-gather.7.cloned.1.call-update
  8.7 0.0 reduce-scatter.2.cloned.1.call-start
  8.7 0.8 reshape.232
  9.5 0.7 fusion.67
  10.2 1.6 convert_reduce_fusion.1
  11.8 0.7 fusion.66
  12.6 2.1 convert_reduce_fusion
  14.7 0.0 copy-done
  14.7 0.0 copy-done.1
  14.7 0.0 copy-done.7
  14.7 5.5 fusion.18
  20.3 4.3 broadcast_in_dim.60
  24.5 19.8 %scatter_fusion = f32[64,128,256]{2,1,0:T(8,128)} fusion(f32[64,128,256]{2,1,0:T(8,128)} %broadcast_in_dim.60, s32[64]{0:T(128)S(1)} %reshape.232, f32[64,128,256]{2,1,0:T(8,128)} %bitcast.77), kind=kCustom, calls=%fused_computation.4 | custom fusion | flops 2097152 | bytes 25166080 | tf_op jit(solution)/shard_map/scatter-add | solution.py:95
  44.3 6.0 %convert_element_type.51 = bf16[64,128,256]{2,1,0:T(8,128)(2,1)} convert(f32[64,128,256]{2,1,0:T(8,128)} %scatter_fusion) | non-fusion elementwise | flops 2097152 | bytes 12582912 | tf_op jit(solution)/shard_map/convert_element_type | solution.py:97
  50.3 0.0 copy-start.9
  50.3 0.0 reduce-scatter.2.cloned.1.call-update
  50.3 0.0 all-gather.9.cloned.1.call-start
  50.4 0.6 copy-done.10
  51.0 0.1 reshape.186
  51.1 0.1 copy.35
  51.1 0.1 mul.58
  51.2 0.1 copy.36
  51.3 0.1 reshape.187
  51.4 0.1 copy.34
  51.6 1.3 fusion.74
  52.9 3.8 gather_fusion
  56.6 66.9 %all-gather.7.cloned.1.call-done = bf16[128,128,128]{2,1,0:T(8,128)(2,1)} async-done(((bf16[4,128,128]{2,1,0:T(8,128)(2,1)}), bf16[128,128,128]{2,1,0:T(8,128)(2,1)}) %all-gather.7.cloned.1.call-update) | async-done | bytes 4194320 | tf_op jit(solution)/shard_map/all_gather | solution.py:50
  123.5 3.8 gather_fusion.1
  127.4 2.2 convolution_bitcast_fusion
  129.6 0.0 copy-done.4
  129.6 0.8 fusion.51
  130.4 0.4 copy-done.6
  130.8 1.5 multiply_convert_fusion
  132.3 0.0 all-gather.9.cloned.1.call-update
  132.3 0.0 all-gather.11.cloned.1.call-start
  132.4 0.5 all-gather.11.cloned.1.call-update
  132.9 0.0 all-reduce.3.cloned.1.call-start
  133.0 2.1 fusion.77
  135.1 28.5 %reduce-scatter.2.cloned.1.call-done = bf16[8,128,256]{2,1,0:T(8,128)(2,1)} async-done(((bf16[64,128,256]{2,1,0:T(8,128)(2,1)}), bf16[8,128,256]{2,1,0:T(8,128)(2,1)}) %reduce-scatter.2.cloned.1.call-update) | async-done | bytes 524304 | tf_op jit(solution)/shard_map/reduce_scatter | solution.py:96
  163.6 2.0 fusion.26
  165.5 0.9 fusion.76
  166.5 1.0 convolution_bitcast_fusion.2
  167.5 35.4 %all-gather.9.cloned.1.call-done = bf16[64,128,256]{2,1,0:T(8,128)(2,1)} async-done(((bf16[8,128,256]{2,1,0:T(8,128)(2,1)}), bf16[64,128,256]{2,1,0:T(8,128)(2,1)}) %all-gather.9.cloned.1.call-update) | async-done | bytes 4194320 | tf_op jit(solution)/shard_map/all_gather | solution.py:70
  202.9 5.0 gather_fusion.2
  207.8 4.2 fusion.13
  212.0 90.8 %all-gather.11.cloned.1.call-done = bf16[128,128,256]{2,1,0:T(8,128)(2,1)} async-done(((bf16[4,128,256]{2,1,0:T(8,128)(2,1)}), bf16[128,128,256]{2,1,0:T(8,128)(2,1)}) %all-gather.11.cloned.1.call-update) | async-done | bytes 8388624 | tf_op jit(solution)/shard_map/all_gather | solution.py:51
  302.8 5.4 gather_fusion.3
  308.2 2.5 divide_convert_fusion
  310.7 0.0 copy-start.2
  310.7 1.0 convolution_bitcast_fusion.1
  311.8 0.0 all-reduce.3.cloned.1.call-update
  311.8 0.3 fusion.75
  312.1 1.1 fusion.25
  313.2 250.1 %all-reduce.3.cloned.1.call-done = (f32[128,256]{0,1:T(8,128)}, f32[128,256]{1,0:T(8,128)}, f32[256,256]{1,0:T(8,128)}, f32[256,256]{1,0:T(8,128)}) async-done(((f32[128,256]{0,1:T(8,128)}, f32[128,256]{1,0:T(8,128)}, f32[256,256]{1,0:T(8,128)}, f32[256,256]{1,0:T(8,128)}), (f32[128,256]{0,1:T(8,128)}, f32[128,256]{1,0:T(8,128)}, f32[256,256]{1,0:T(8,128)}, ...) | async-done | bytes 786448 | tf_op jit(solution)/shard_map/psum | solution.py:107
  563.3 1.7 copy.40
  564.9 1.6 copy.53
  566.5 1.7 copy.54
  568.2 1.7 copy.55
  (26 shorter events, 0.1 us)
Async XLA Ops:
  7.2 7.6 %copy-start = (bf16[8,128,256]{2,1,0:T(8,128)(2,1)S(1)}, bf16[8,128,256]{2,1,0:T(8,128)(2,1)}, u32[]{:S(2)}) copy-start(bf16[8,128,256]{2,1,0:T(8,128)(2,1)} %param.29) | copy-start | bytes 1572868
  7.2 7.5 %copy-start.1 = (bf16[8,8,128,128]{3,2,1,0:T(8,128)(2,1)S(1)}, bf16[8,8,128,128]{3,2,1,0:T(8,128)(2,1)}, u32[]{:S(2)}) copy-start(bf16[8,8,128,128]{3,2,1,0:T(8,128)(2,1)} %param.18) | copy-start | bytes 6291460
  7.2 7.5 %copy-start.7 = (bf16[256,256]{1,0:T(8,128)(2,1)S(1)}, bf16[256,256]{1,0:T(8,128)(2,1)}, u32[]{:S(2)}) copy-start(bf16[256,256]{1,0:T(8,128)(2,1)} %param.28) | copy-start | bytes 393220
  7.2 45.7 %all-gather.5.cloned.1.call-start = ((), (), s32[]{:S(2)}) async-start(), calls=%async_computation.1 | async-start | bytes 2359296 | tf_op jit(solution)/shard_map/all_gather | solution.py:59
  7.9 115.6 %all-gather.7.cloned.1.call-start = ((), (), s32[]{:S(2)}) async-start(), calls=%async_computation.2 | async-start | bytes 4325376 | tf_op jit(solution)/shard_map/all_gather | solution.py:50
  8.7 154.9 %reduce-scatter.2.cloned.1.call-start = ((), (), s32[]{:S(2)}) async-start(), calls=%async_computation.5 | async-start | bytes 4718592 | tf_op jit(solution)/shard_map/reduce_scatter | solution.py:96
  50.3 0.7 copy-start.10
  50.3 0.8 copy-start.12
  50.3 0.9 copy-start.11
  50.3 1.3 copy-start.3
  50.3 1.3 copy-start.9
  50.3 152.5 %all-gather.9.cloned.1.call-start = ((), (), s32[]{:S(2)}) async-start(), calls=%async_computation.3 | async-start | bytes 4718592 | tf_op jit(solution)/shard_map/all_gather | solution.py:70
  127.4 2.2 copy-start.4
  129.6 1.2 copy-start.6
  129.6 1.2 copy-start.13
  132.3 31.3 %copy-start.8 = (bf16[256,256]{1,0:T(8,128)(2,1)S(1)}, bf16[256,256]{1,0:T(8,128)(2,1)}, u32[]{:S(2)}) copy-start(bf16[256,256]{1,0:T(8,128)(2,1)} %param.27) | copy-start | bytes 393220
  132.3 170.4 %all-gather.11.cloned.1.call-start = ((), (), s32[]{:S(2)}) async-start(), calls=%async_computation.4 | async-start | bytes 8650752 | tf_op jit(solution)/shard_map/all_gather | solution.py:51
  132.9 430.3 %all-reduce.3.cloned.1.call-start = ((), (), s32[]{:S(2)}) async-start(), calls=%async_computation.6 | async-start | bytes 1572864 | tf_op jit(solution)/shard_map/psum | solution.py:107
  212.0 96.2 %copy-start.5 = (bf16[8,4,128,128]{3,2,1,0:T(8,128)(2,1)S(1)}, bf16[8,4,128,128]{3,2,1,0:T(8,128)(2,1)}, u32[]{:S(2)}) copy-start(bf16[8,4,128,128]{3,2,1,0:T(8,128)(2,1)} %param.22) | copy-start | bytes 3145732
  310.7 1.1 copy-start.2
Sparse Core Ops, SparseCore 0:
  9.9 31.9 all-gather.4
  44.5 79.0 all-gather.6
  126.1 37.4 reduce-scatter.1
  165.9 36.9 all-gather.8
  205.3 97.4 all-gather.10
  311.9 251.3 all-reduce.2
where the time goes:
time: 578 us; the launch traced here: 577 us
  waiting for transfers between devices  474 us (82%)
  local copies, waits for them, and re-layouts  31.2 us (5%)
  other arithmetic  31 us (5%)
  matrix products  26.4 us (5%)
  between operations  14.3 us (2%)
    psum x1, waiting for transfers between devices, body(): lax.psum((grad_self_one, grad_neigh_one, grad_self_two, grad_neigh_two),...  250 us
    all_gather x1, waiting for transfers between devices, body(): lax.all_gather(hidden_store, 'wide', axis=0, tiled=True)  90.8 us
    all_gather x1, waiting for transfers between devices, body(): lax.all_gather(feature_store, 'wide', axis=0, tiled=True)  66.9 us
    all_gather x1, waiting for transfers between devices, body(): lax.all_gather(hidden.reshape(clusters, block, width_hid), 'grp', axis=0,...  35.4 us
    reduce_scatter x1, waiting for transfers between devices, body(): lax.psum_scatter(by_target.astype(jnp.bfloat16), 'grp', scatter_dimension...  28.5 us
    scatter-add x1, other arithmetic, body(): jax.ops.segment_sum(slot_terms, sources, num_segments=group_rows)  19.8 us
  transfers between devices with their start and end apart: 6, of which 5 were waited for; matrix products, arithmetic and copies ran while one was open for 12% of the time, Pallas kernels for 0%

commit v1 on v0

v1 whole, which is shorter than its diff:
```python
import jax
import jax.numpy as jnp
from jax import lax
from jax.experimental import pallas as pl
from jax.experimental.pallas import tpu as pltpu
from jax.sharding import PartitionSpec as P

MESH = pl.DeviceIdType.MESH
F32 = jnp.float32
BF16 = jnp.bfloat16
NX, NY, NZ = 4, 4, 8


def prep_kernel(gsrc, gcnt, howner, hlocal, hcnt, out, seen, start):
    @pl.loop(0, 64)
    def _(i):
        seen[i] = 0

    @pl.loop(0, 8)
    def _(k):
        for s in range(8):
            t = gsrc[k, s]
            out[5, k * 8 + s] = t
            seen[t] = seen[t] + 1
        for s in range(4):
            out[6, k * 4 + s] = howner[k, s, 0] * 4 + hlocal[k, s]
        out[7, k] = gcnt[k]
        out[7, 8 + k] = hcnt[k]

    def scan(g, base):
        start[g] = base
        many = seen[g]
        out[3, g] = jnp.maximum(base + many - 1, 0)
        out[4, g] = jnp.minimum(many, 1)
        seen[g] = 0
        return base + many

    lax.fori_loop(0, 64, scan, jnp.int32(0))

    @pl.loop(0, 8)
    def _(k):
        for s in range(8):
            t = gsrc[k, s]
            place = start[t] + seen[t]
            out[0, place] = k * 8 + s
            out[1, place] = k
            out[2, place] = jnp.minimum(seen[t], 1)
            seen[t] = seen[t] + 1


def prep(gsrc, gcnt, howner, hlocal, hcnt):
    smem = pl.BlockSpec(memory_space=pltpu.SMEM)
    return pl.pallas_call(
        prep_kernel,
        out_shape=jax.ShapeDtypeStruct((8, 64), jnp.int32),
        in_specs=[smem] * 5,
        out_specs=smem,
        scratch_shapes=[pltpu.SMEM((64,), jnp.int32), pltpu.SMEM((64,), jnp.int32)],
    )(gsrc, gcnt, howner, hlocal, hcnt)


def dot(a, b):
    return jnp.dot(a, b, preferred_element_type=F32)


def dot_t(a, b):
    return lax.dot_general(a, b, (((0,), (0,)), ((), ())), preferred_element_type=F32)


def dot_nt(a, b):
    return lax.dot_general(a, b, (((1,), (1,)), ((), ())), preferred_element_type=F32)


def main_kernel(
    sc, features, gtiles, htiles, fstore, hstore, s1_h, n1_h, s2_h, n2_h, cot_h,
    emb, gs1, gn1, gs2, gn2,
    GF, GM, GH, HF, HH, TA, TB, COT, S1, N1, S2, N2,
    INV, SC, RT, PS, PR, Q, T1, FR, RB, ACC, PRE, HO, FAR, MF,
    G, GP, B1, Q1, B2, Q2, B3, B4, FG,
    load_sem, ysem_s, ysem_r, sib_s, sib_r, axs, axr, azs, azr, bzs, bzr, bxs, bxr,
    rs_s, rs_r, ps_s, ps_r, a_s, a_r, b2s, b2r, b3s, b3r, b4s, b4r, b5s, b5r, b6s, b6r,
):
    grp = lax.axis_index("grp")
    wide = lax.axis_index("wide")
    z, x = wide // NX, wide % NX
    y, c = grp // 2, grp % 2
    o = 1 - c

    def at(dz=0, dy=0, dx=0):
        return (((y + dy) % NY) * 2 + c, ((z + dz) % NZ) * NX + (x + dx) % NX)

    sib = (y * 2 + o, wide)
    pending = []

    def send(src, dst, ss, rs, dev):
        cp = pltpu.make_async_remote_copy(
            src_ref=src, dst_ref=dst, send_sem=ss, recv_sem=rs, device_id=dev, device_id_type=MESH
        )
        cp.start()
        pending.append(cp)

    def sib_send(ref, index):
        pltpu.make_async_remote_copy(
            src_ref=ref, dst_ref=ref, send_sem=sib_s.at[index], recv_sem=sib_r.at[index],
            device_id=sib, device_id_type=MESH,
        ).start()

    def arrive(dst, rs, ss):
        pltpu.make_async_remote_copy(
            src_ref=dst, dst_ref=dst, send_sem=ss, recv_sem=rs, device_id=sib, device_id_type=MESH
        ).wait_recv()

    def sib_wait(ref, index):
        pltpu.make_async_remote_copy(
            src_ref=ref, dst_ref=ref, send_sem=sib_s.at[index], recv_sem=sib_r.at[index],
            device_id=sib, device_id_type=MESH,
        ).wait()

    partners = [sib]
    partners += [at(dy=d) for d in range(1, NY)]
    partners += [at(dx=d) for d in range(1, NX)]
    partners += [at(dz=d) for d in range(1, NZ)]
    barrier = pltpu.get_barrier_semaphore()
    for p in partners:
        pl.semaphore_signal(barrier, inc=1, device_id=p, device_id_type=MESH)

    own = pl.ds(grp * 8, 8)
    loads = []

    def load(src, dst):
        cp = pltpu.make_async_copy(src, dst, load_sem.at[len(loads)])
        cp.start()
        loads.append(cp)
        return cp

    l_ft = load(features, GF.at[own])
    l_fs = load(fstore.at[pl.ds(2 * c, 2)], HF.at[z, x, pl.ds(2 * c, 2)])
    l_hs = load(hstore.at[pl.ds(2 * c, 2)], HH.at[z, x, pl.ds(2 * c, 2)])
    l_ta = load(gtiles, TA)
    l_tb = load(htiles, TB)
    l_ct = load(cot_h, COT)
    l_w = [load(s1_h, S1), load(n1_h, N1), load(s2_h, S2), load(n2_h, N2)]

    la, lb = 2 * c, 2 * c + 1
    LOW, HIGH = pl.ds(0, 64), pl.ds(64, 64)

    def zz(d):
        return (z + d) % NZ

    def xx(d):
        return (x + d) % NX

    def a_x1(X, n):
        r = X.at[z, x, la]
        send(r, r, axs.at[n, 0], axr.at[n, 0], at(dx=1))
        send(r, r, axs.at[n, 1], axr.at[n, 1], at(dx=-1))

    def a_x1_in(X, n):
        arrive(X.at[z, xx(-1), la], axr.at[n, 0], axs.at[n, 0])
        arrive(X.at[z, xx(1), la], axr.at[n, 1], axs.at[n, 1])

    def a_x2(X, n):
        r = X.at[z, xx(-1), la, LOW]
        send(r, r, axs.at[n, 2], axr.at[n, 2], at(dx=1))
        r = X.at[z, xx(1), la, HIGH]
        send(r, r, axs.at[n, 3], axr.at[n, 3], at(dx=-1))

    def a_x2_in(X, n):
        arrive(X.at[z, xx(2), la, LOW], axr.at[n, 2], axs.at[n, 2])
        arrive(X.at[z, xx(2), la, HIGH], axr.at[n, 3], axs.at[n, 3])

    def every_x(X, zi, l, part):
        return X.at[zi, pl.ds(0, NX), l] if part is None else X.at[zi, pl.ds(0, NX), l, part]

    def a_z(X, n, j):
        low, high = (LOW, HIGH) if j == 4 else (None, None)
        r = every_x(X, zz(-(j - 1)), la, low)
        send(r, r, azs.at[n, 2 * j - 2], azr.at[n, 2 * j - 2], at(dz=1))
        r = every_x(X, zz(j - 1), la, high)
        send(r, r, azs.at[n, 2 * j - 1], azr.at[n, 2 * j - 1], at(dz=-1))

    def a_z_in(X, n, j):
        low, high = (LOW, HIGH) if j == 4 else (None, None)
        arrive(every_x(X, zz(-j), la, low), azr.at[n, 2 * j - 2], azs.at[n, 2 * j - 2])
        arrive(every_x(X, zz(j), la, high), azr.at[n, 2 * j - 1], azs.at[n, 2 * j - 1])

    def one(X, zi, xi, l, part):
        return X.at[zi, xi, l] if part is None else X.at[zi, xi, l, part]

    def b_z(X, n, j):
        low, high = (LOW, HIGH) if j == 4 else (None, None)
        r = one(X, zz(-(j - 1)), x, lb, low)
        send(r, r, bzs.at[n, 2 * j - 2], bzr.at[n, 2 * j - 2], at(dz=1))
        r = one(X, zz(j - 1), x, lb, high)
        send(r, r, bzs.at[n, 2 * j - 1], bzr.at[n, 2 * j - 1], at(dz=-1))

    def b_z_in(X, n, j):
        low, high = (LOW, HIGH) if j == 4 else (None, None)
        arrive(one(X, zz(-j), x, lb, low), bzr.at[n, 2 * j - 2], bzs.at[n, 2 * j - 2])
        arrive(one(X, zz(j), x, lb, high), bzr.at[n, 2 * j - 1], bzs.at[n, 2 * j - 1])

    def b_x1(X, n, ds):
        for d in ds:
            r = X.at[zz(d), x, lb]
            e = d % NZ
            send(r, r, bxs.at[n, 4 * e], bxr.at[n, 4 * e], at(dx=1))
            send(r, r, bxs.at[n, 4 * e + 1], bxr.at[n, 4 * e + 1], at(dx=-1))

    def b_x1_in_x2(X, n, ds):
        for d in ds:
            e = d % NZ
            arrive(X.at[zz(d), xx(-1), lb], bxr.at[n, 4 * e], bxs.at[n, 4 * e])
            r = X.at[zz(d), xx(-1), lb, LOW]
            send(r, r, bxs.at[n, 4 * e + 2], bxr.at[n, 4 * e + 2], at(dx=1))
            arrive(X.at[zz(d), xx(1), lb], bxr.at[n, 4 * e + 1], bxs.at[n, 4 * e + 1])
            r = X.at[zz(d), xx(1), lb, HIGH]
            send(r, r, bxs.at[n, 4 * e + 3], bxr.at[n, 4 * e + 3], at(dx=-1))

    def b_x2_in(X, n, ds):
        for d in ds:
            e = d % NZ
            arrive(X.at[zz(d), xx(2), lb, LOW], bxr.at[n, 4 * e + 2], bxs.at[n, 4 * e + 2])
            arrive(X.at[zz(d), xx(2), lb, HIGH], bxr.at[n, 4 * e + 3], bxs.at[n, 4 * e + 3])
            sib_send(every_x(X, zz(d), lb, None), n)

    def a_share(X, n, ds):
        for d in ds:
            sib_send(every_x(X, zz(d), la, None), n)

    def plane(X, n, r):
        if r == 0:
            a_x1(X, n)
            b_z(X, n, 1)
            b_x1(X, n, (0,))
        elif r == 1:
            a_x1_in(X, n)
            a_x2(X, n)
            b_z_in(X, n, 1)
            b_z(X, n, 2)
            b_x1(X, n, (-1, 1))
            b_x1_in_x2(X, n, (0,))
        elif r == 2:
            a_x2_in(X, n)
            a_z(X, n, 1)
            b_z_in(X, n, 2)
            b_z(X, n, 3)
            b_x1(X, n, (-2, 2))
            b_x1_in_x2(X, n, (-1, 1))
            b_x2_in(X, n, (0,))
            a_share(X, n, (0,))
        elif r == 3:
            a_z_in(X, n, 1)
            a_z(X, n, 2)
            b_z_in(X, n, 3)
            b_z(X, n, 4)
            b_x1(X, n, (-3, 3))
            b_x1_in_x2(X, n, (-2, 2))
            b_x2_in(X, n, (-1, 1))
            a_share(X, n, (-1, 1))
        elif r == 4:
            b_z_in(X, n, 4)
            b_x1(X, n, (4,))
            a_z_in(X, n, 2)
            a_z(X, n, 3)
            b_x1_in_x2(X, n, (-3, 3))
            b_x2_in(X, n, (-2, 2))
            a_share(X, n, (-2, 2))
        elif r == 5:
            b_x1_in_x2(X, n, (4,))
            a_z_in(X, n, 3)
            a_z(X, n, 4)
            b_x2_in(X, n, (-3, 3))
            a_share(X, n, (-3, 3))
        else:
            b_x2_in(X, n, (4,))
            a_z_in(X, n, 4)
            a_share(X, n, (4,))

    def plane_done(X, n):
        sib_wait(X.at[:, :, pl.ds(2 * o, 2)], n)

    def chunk(X, d, first=0, many=8):
        return X.at[pl.ds((((y + d) % NY) * 2 + c) * 8 + first, many)]

    def ring(X, n, r):
        if r == 0:
            q = chunk(X, 0)
            send(q, q, ysem_s.at[n, 0], ysem_r.at[n, 0], at(dy=1))
            send(q, q, ysem_s.at[n, 1], ysem_r.at[n, 1], at(dy=-1))
            sib_send(q, 2 + n)
        elif r == 1:
            q = chunk(X, -1)
            arrive(q, ysem_r.at[n, 0], ysem_s.at[n, 0])
            h = chunk(X, -1, 0, 4)
            send(h, h, ysem_s.at[n, 2], ysem_r.at[n, 2], at(dy=1))
            sib_send(q, 2 + n)
            q = chunk(X, 1)
            arrive(q, ysem_r.at[n, 1], ysem_s.at[n, 1])
            h = chunk(X, 1, 4, 4)
            send(h, h, ysem_s.at[n, 3], ysem_r.at[n, 3], at(dy=-1))
            sib_send(q, 2 + n)
        else:
            arrive(chunk(X, 2, 0, 4), ysem_r.at[n, 2], ysem_s.at[n, 2])
            arrive(chunk(X, 2, 4, 4), ysem_r.at[n, 3], ysem_s.at[n, 3])
            sib_send(chunk(X, 2), 2 + n)

    def ring_done(X, n):
        sib_wait(X.at[pl.ds(0, 32)], 2 + n)

    l_fs.wait()
    l_ft.wait()
    l_hs.wait()
    pl.semaphore_wait(barrier, len(partners))
    plane(HF, 0, 0)
    ring(GF, 0, 0)
    plane(HH, 1, 0)
    l_ta.wait()
    l_tb.wait()
    l_ct.wait()

    @pl.loop(0, 8)
    def _(k):
        near_live, far_live = sc[7, k], sc[7, 8 + k]
        total = jnp.zeros((128, 128), F32)
        for s in range(8):
            t = TA[k * 8 + s].astype(F32) * jnp.where(s < near_live, 1.0, 0.0)
            TA[k * 8 + s] = t.astype(BF16)
            total = total + t
        for s in range(4):
            t = TB[k * 4 + s].astype(F32) * jnp.where(s < far_live, 1.0, 0.0)
            TB[k * 4 + s] = t.astype(BF16)
            total = total + t
        inv = 1.0 / (1.0 + jnp.sum(total, axis=1, keepdims=True))
        INV[k] = jnp.broadcast_to(inv, (128, 128))
        SC[k] = (COT[k].astype(F32) * inv).astype(BF16)

    plane(HF, 0, 1)

    def term(i, acc):
        acc = acc * sc[2, i].astype(F32) + dot_t(TA[sc[0, i]], SC[sc[1, i]])
        RT[i] = acc.astype(BF16)
        return acc

    acc = lax.fori_loop(0, 32, term, jnp.zeros((128, 256), F32))
    plane(HH, 1, 1)
    plane(HF, 0, 2)
    acc = lax.fori_loop(32, 64, term, acc)
    ring(GF, 0, 1)

    @pl.loop(0, 32)
    def _(i):
        g = ((i // 8) * 2 + o) * 8 + i % 8
        PS[i] = (RT[sc[3, g]].astype(F32) * sc[4, g].astype(F32)).astype(BF16)

    send(PS, PR, ps_s, ps_r, sib)
    plane(HF, 0, 3)
    plane(HH, 1, 2)
    ring(GF, 0, 2)
    arrive(PR, ps_r, ps_s)

    @pl.loop(0, 32)
    def _(i):
        g = ((i // 8) * 2 + c) * 8 + i % 8
        v = RT[sc[3, g]].astype(F32) * sc[4, g].astype(F32) + PR[i].astype(F32)
        Q[i] = v.astype(BF16)

    def piece(d, first):
        return Q.at[pl.ds(((y + d) % NY) * 8 + first, 4)]

    send(piece(2, 0), T1.at[0], rs_s.at[0], rs_r.at[0], at(dy=1))
    send(piece(2, 4), T1.at[1], rs_s.at[1], rs_r.at[1], at(dy=-1))
    send(piece(1, 4), FR.at[0, pl.ds(4, 4)], rs_s.at[2], rs_r.at[2], at(dy=1))
    send(piece(-1, 0), FR.at[1, pl.ds(0, 4)], rs_s.at[3], rs_r.at[3], at(dy=-1))
    plane(HF, 0, 4)
    ring_done(GF, 0)

    @pl.loop(0, 8)
    def _(k):
        total = jnp.zeros((128, 128), F32)
        for s in range(8):
            total = total + dot(TA[k * 8 + s], GF[sc[5, k * 8 + s]])
        ACC[k] = total

    plane(HF, 0, 5)
    plane(HH, 1, 3)
    for w in l_w:
        w.wait()
    plane(HF, 0, 6)
    plane_done(HF, 0)

    @pl.loop(0, 8)
    def _(k):
        total = ACC[k]
        for s in range(4):
            f = sc[6, k * 4 + s]
            total = total + dot(TB[k * 4 + s], HF[f // 16, (f // 4) % 4, f % 4])
        mean = (total * INV[k]).astype(BF16)
        GM[grp * 8 + k] = mean
        pre = dot(GF[grp * 8 + k], S1[...]) + dot(mean, N1[...])
        PRE[k] = pre
        HO[k] = (pre * jax.nn.sigmoid(pre)).astype(BF16)

    ring(GM, 1, 0)
    plane(HH, 1, 4)

    arrive(T1.at[0], rs_r.at[0], rs_s.at[0])

    @pl.loop(0, 4)
    def _(i):
        j = ((y + 1) % NY) * 8 + i
        Q[j] = (Q[j].astype(F32) + T1[0, i].astype(F32)).astype(BF16)

    send(piece(1, 0), FR.at[0, pl.ds(0, 4)], rs_s.at[4], rs_r.at[4], at(dy=1))
    arrive(T1.at[1], rs_r.at[1], rs_s.at[1])

    @pl.loop(0, 4)
    def _(i):
        j = ((y + 3) % NY) * 8 + 4 + i
        Q[j] = (Q[j].astype(F32) + T1[1, i].astype(F32)).astype(BF16)

    send(piece(-1, 4), FR.at[1, pl.ds(4, 4)], rs_s.at[5], rs_r.at[5], at(dy=-1))

    def put(first, rows, v):
        G[pl.ds(first, rows), :] = v[:, :128].astype(BF16)
        G[pl.ds(first + rows, rows), :] = v[:, 128:].astype(BF16)

    GP[...] = jnp.zeros_like(GP)

    @pl.loop(0, 8)
    def _(k):
        GP[...] = GP[...] + dot_t(HO[k], COT[k])

    put(512, 256, GP[...])
    plane(HH, 1, 5)
    ring(GM, 1, 1)
    plane(HH, 1, 6)
    plane_done(HH, 1)

    GP[...] = jnp.zeros_like(GP)

    @pl.loop(0, 8)
    def _(k):
        total = jnp.zeros((128, 256), F32)
        for s in range(4):
            f = sc[6, k * 4 + s]
            total = total + dot(TB[k * 4 + s], HH[f // 16, (f // 4) % 4, f % 4])
        FAR[k] = total
        inv = INV[k]
        m = jnp.concatenate([total[:, :128] * inv, total[:, 128:] * inv], axis=1).astype(BF16)
        GP[...] = GP[...] + dot_t(m, COT[k])

    ring(GM, 1, 2)
    arrive(FR.at[0, pl.ds(4, 4)], rs_r.at[2], rs_s.at[2])
    arrive(FR.at[1, pl.ds(0, 4)], rs_r.at[3], rs_s.at[3])
    arrive(FR.at[0, pl.ds(0, 4)], rs_r.at[4], rs_s.at[4])
    arrive(FR.at[1, pl.ds(4, 4)], rs_r.at[5], rs_s.at[5])

    MF[...] = jnp.zeros_like(MF)

    @pl.loop(0, 8)
    def _(k):
        r = Q[y * 8 + k].astype(F32) + FR[0, k].astype(F32) + FR[1, k].astype(F32)
        r = r.astype(BF16)
        GP[...] = GP[...] + dot_t(HO[k], r)
        total = dot_nt(COT[k], S2[...]) + dot_nt(r, N2[...])
        pre = PRE[k]
        sigma = jax.nn.sigmoid(pre)
        gp = (total * sigma * (1.0 + pre * (1.0 - sigma))).astype(BF16)
        MF[0] = MF[0] + dot_t(GF[grp * 8 + k], gp)
        MF[1] = MF[1] + dot_t(GM[grp * 8 + k], gp)

    put(1024, 256, GP[...])
    put(0, 128, MF[0])
    put(256, 128, MF[1])

    send(G.at[pl.ds(o * 768, 768)], B1, a_s.at[0], a_r.at[0], sib)
    ring_done(GM, 1)

    def group_hidden(first, many):
        @pl.loop(first, first + many)
        def _(j):
            pre = dot(GF[j], S1[...]) + dot(GM[j], N1[...])
            GH[j] = (pre * jax.nn.sigmoid(pre)).astype(BF16)

    arrive(B1, a_r.at[0], a_s.at[0])
    Q1[...] = (G[pl.ds(c * 768, 768), :].astype(F32) + B1[...].astype(F32)).astype(BF16)
    for d in range(1, NY):
        send(Q1.at[pl.ds(((y + d) % NY) * 192, 192)], B2.at[d - 1], b2s.at[d - 1], b2r.at[d - 1], at(dy=d))
    group_hidden(0, 32)
    for d in range(1, NY):
        arrive(B2.at[d - 1], b2r.at[d - 1], b2s.at[d - 1])
    Q2[...] = (
        Q1[pl.ds(y * 192, 192), :].astype(F32) + B2[0].astype(F32) + B2[1].astype(F32) + B2[2].astype(F32)
    ).astype(BF16)
    for d in range(1, NX):
        send(Q2.at[pl.ds(((x + d) % NX) * 48, 48)], B3.at[d - 1], b3s.at[d - 1], b3r.at[d - 1], at(dx=d))
    group_hidden(32, 32)
    for d in range(1, NX):
        arrive(B3.at[d - 1], b3r.at[d - 1], b3s.at[d - 1])
    B4[z] = (
        Q2[pl.ds(x * 48, 48), :].astype(F32) + B3[0].astype(F32) + B3[1].astype(F32) + B3[2].astype(F32)
    ).astype(BF16)
    for d in range(1, NZ):
        send(B4.at[z], B4.at[z], b4s.at[d - 1], b4r.at[d - 1], at(dz=d))

    @pl.loop(0, 8)
    def _(k):
        total = FAR[k]
        for s in range(8):
            total = total + dot(TA[k * 8 + s], GH[sc[5, k * 8 + s]])
        inv = INV[k]
        m = jnp.concatenate([total[:, :128] * inv, total[:, 128:] * inv], axis=1).astype(BF16)
        emb[k] = (dot(HO[k], S2[...]) + dot(m, N2[...])).astype(BF16)

    for d in range(1, NZ):
        arrive(B4.at[zz(-d)], b4r.at[d - 1], b4s.at[d - 1])
    total = B4[0].astype(F32)
    for i in range(1, NZ):
        total = total + B4[i].astype(F32)
    mine = pl.ds(c * 768 + y * 192 + x * 48, 48)
    FG[mine, :] = total.astype(BF16)
    for d in range(1, NX):
        send(FG.at[mine], FG.at[mine], b5s.at[d - 1], b5r.at[d - 1], at(dx=d))
    for d in range(1, NX):
        arrive(FG.at[pl.ds(c * 768 + y * 192 + xx(-d) * 48, 48)], b5r.at[d - 1], b5s.at[d - 1])
    row = FG.at[pl.ds(c * 768 + y * 192, 192)]
    for d in range(1, NY):
        send(row, row, b6s.at[d - 1], b6r.at[d - 1], at(dy=d))
    for d in range(1, NY):
        arrive(FG.at[pl.ds(c * 768 + ((y - d) % NY) * 192, 192)], b6r.at[d - 1], b6s.at[d - 1])
    half = FG.at[pl.ds(c * 768, 768)]
    send(half, half, a_s.at[1], a_r.at[1], sib)
    arrive(FG.at[pl.ds(o * 768, 768)], a_r.at[1], a_s.at[1])

    def take(first, rows, out):
        out[:, :128] = FG[pl.ds(first, rows), :].astype(F32)
        out[:, 128:] = FG[pl.ds(first + rows, rows), :].astype(F32)

    take(0, 128, gs1)
    take(256, 128, gn1)
    take(512, 256, gs2)
    take(1024, 256, gn2)
    for cp in pending:
        cp.wait_send()


def body(
    features, group_src, group_count, group_tiles, hist_owner, hist_local, hist_count, hist_tiles,
    feature_store, hidden_store, self_one, neigh_one, self_two, neigh_two, cotangent,
):
    scalars = prep(group_src, group_count, hist_owner, hist_local, hist_count)
    anywhere = pl.BlockSpec(memory_space=pl.ANY)
    vmem = pl.BlockSpec(memory_space=pltpu.VMEM)
    V, D, R = pltpu.VMEM, pltpu.SemaphoreType.DMA, pltpu.SemaphoreType.REGULAR
    scratch = [
        V((64, 128, 128), BF16), V((64, 128, 128), BF16), V((64, 128, 256), BF16),
        V((8, 4, 4, 128, 128), BF16), V((8, 4, 4, 128, 256), BF16),
        V((64, 128, 128), BF16), V((32, 128, 128), BF16), V((8, 128, 256), BF16),
        V((128, 256), BF16), V((128, 256), BF16), V((256, 256), BF16), V((256, 256), BF16),
        V((8, 128, 128), F32), V((8, 128, 256), BF16), V((64, 128, 256), BF16),
        V((32, 128, 256), BF16), V((32, 128, 256), BF16), V((32, 128, 256), BF16),
        V((2, 4, 128, 256), BF16), V((2, 8, 128, 256), BF16), V((8, 128, 256), BF16),
        V((8, 128, 128), F32), V((8, 128, 256), F32), V((8, 128, 256), BF16),
        V((8, 128, 256), F32), V((2, 128, 256), F32),
        V((1536, 128), BF16), V((256, 256), F32), V((768, 128), BF16), V((768, 128), BF16),
        V((3, 192, 128), BF16), V((192, 128), BF16), V((3, 48, 128), BF16), V((8, 48, 128), BF16),
        V((1536, 128), BF16),
        D((10,)), D((2, 4)), D((2, 4)), D((4,)), D((4,)),
        D((2, 4)), D((2, 4)), D((2, 8)), D((2, 8)), D((2, 8)), D((2, 8)), D((2, 32)), D((2, 32)),
        D((6,)), D((6,)), D, D, D((2,)), D((2,)),
        D((3,)), D((3,)), D((3,)), D((3,)), D((7,)), D((7,)), D((3,)), D((3,)), D((3,)), D((3,)),
    ]
    return pl.pallas_call(
        main_kernel,
        out_shape=(
            jax.ShapeDtypeStruct((8, 128, 256), BF16),
            jax.ShapeDtypeStruct((128, 256), F32),
            jax.ShapeDtypeStruct((128, 256), F32),
            jax.ShapeDtypeStruct((256, 256), F32),
            jax.ShapeDtypeStruct((256, 256), F32),
        ),
        in_specs=[pl.BlockSpec(memory_space=pltpu.SMEM)] + [anywhere] * 10,
        out_specs=(vmem,) * 5,
        scratch_shapes=scratch,
        compiler_params=pltpu.CompilerParams(
            collective_id=0, has_side_effects=True, vmem_limit_bytes=60 * 2**20
        ),
    )(
        scalars, features, group_tiles.reshape(64, 128, 128), hist_tiles.reshape(32, 128, 128),
        feature_store, hidden_store, self_one, neigh_one, self_two, neigh_two, cotangent,
    )


def solution(mesh):
    every = P(("grp", "wide"))
    wide = P("wide")
    placed = (every,) * 8 + (wide, wide) + (P(),) * 4 + (every,)
    return jax.shard_map(
        body, mesh=mesh, in_specs=placed, out_specs=(every, P(), P(), P(), P()), check_vma=False
    )
```

time: 578 us -> 122 us (0.21)
  waiting for transfers between devices: 474 us -> 0 us
  Pallas kernels: 0 us -> 111 us
  other arithmetic: 31 us -> 0 us
  matrix products: 26.4 us -> 0 us
  local copies, waits for them, and re-layouts: 31.2 us -> 10.1 us
  between operations: 14.3 us -> 0.66 us
    psum x1 -> x0, waiting for transfers between devices: 250 us -> none  [body(): lax.psum((grad_self_one, grad_neigh_one, grad_self_two, grad_neigh_two),...]
    all_gather x4 -> x0, waiting for transfers between devices: 193 us -> none  [the longest x1 90.8 us: body(): lax.all_gather(hidden_store, 'wide', axis=0, tiled=True)]
    pallas_call x0 -> x2, Pallas kernels: none -> 111 us  [the longest x1 107 us: body(): pl.pallas_call(main_kernel, out_shape=(jax.ShapeDtypeStruct((8, 128, 256)...]
    reduce_scatter x1 -> x0, waiting for transfers between devices: 28.5 us -> none  [body(): lax.psum_scatter(by_target.astype(jnp.bfloat16), 'grp', scatter_dimension...]
    dot_general x14 -> x0, matrix products: 26.4 us -> none  [the longest x1 5.54 us: body(): jnp.einsum('csrj,crf->csjf', tiles_near, scaled, preferred_element_type=j...]
    scatter-add x1 -> x0, other arithmetic: 19.8 us -> none  [body(): jax.ops.segment_sum(slot_terms, sources, num_segments=group_rows)]
    gather x4 -> x0, local copies, waits for them, and re-layouts: 18 us -> none  [the longest x1 5.45 us: body(): far_hid = jnp.take(whole_hid, wanted, axis=0)]
    convert_element_type x3 -> x0, other arithmetic: 7.43 us -> none  [the longest x1 5.97 us: body(): by_target.astype(jnp.bfloat16)]
  transfers between devices with their start and end apart: 6 -> 0, of which waited for: 5 -> 0; matrix products, arithmetic and copies ran while one was open for 12% -> 0% of each run, Pallas kernels for 0% -> 0%
where the time goes in v1:
time: 122 us
  Pallas kernels  111 us (91%)
  local copies, waits for them, and re-layouts  10.1 us (8%)
    pallas_call x1, Pallas kernels, body(): pl.pallas_call(main_kernel, out_shape=(jax.ShapeDtypeStruct((8, 128, 256)...  107 us
    unnamed x9, local copies, waits for them, and re-layouts  10.1 us
    pallas_call x1, Pallas kernels, prep(): pl.pallas_call(prep_kernel, out_shape=jax.ShapeDtypeStruct((8, 64), jnp.i...  3.71 us

profile of v1, /device:TPU:1, one launch (start us, length us, event | category | flops | bytes accessed | tf_op | source)
XLA Modules:
  0.0 121.9 jit_solution(10862810192717874738)
XLA Ops:
  0.6 1.3 %copy.21.hlocal = s32[8,4]{1,0:T(8,128)} copy(s32[8,4]{0,1:T(4,128)} %param.20) | data formatting | bytes 256 | tf_op args[5]
  2.0 1.4 %copy.20.howner = s32[8,4,1]{2,1,0:T(4,128)} copy(s32[8,4,1]{0,2,1:T(1,128)} %param.19) | data formatting | bytes 256 | tf_op args[4]
  3.4 3.7 %shard_map.182.sc = s32[8,64]{1,0:T(8,128)} custom-call(s32[8,8]{1,0:T(8,128)} %gsrc.1, s32[8]{0:T(128)} %gcnt.1, s32[8,4,1]{2,1,0:T(4,128)} %copy.20.howner, s32[8,4]{1,0:T(8,128)} %copy.21.hlocal, s32[8]{0:T(128)} %hcnt.1), custom_call_target="tpu_custom_call" | custom-call | tf_op jit(solution)/shard_map/pallas_call | solution.py:53
  7.1 107.4 %shard_map.183 = (bf16[8,128,256]{2,1,0:T(8,128)(2,1)}, f32[128,256]{1,0:T(8,128)}, f32[128,256]{1,0:T(8,128)}, f32[256,256]{1,0:T(8,128)}, f32[256,256]{1,0:T(8,128)}) custom-call(s32[8,64]{1,0:T(8,128)} %shard_map.182.sc, bf16[8,128,128]{2,1,0:T(8,128)(2,1)} %features.1, bf16[64,128,128]{2,1,0:T(8,128)(2,1)} %bitcast.2, bf16[32,128,128]{2,1,0:T(8,128)(2,1)} %bitcast.3, ...), custom_call_target="tpu_custom_call" | custom-call | tf_op jit(solution)/shard_map/pallas_call | solution.py:573
  114.5 0.0 copy-start
  114.5 1.9 %copy.27 = bf16[8,128,256]{2,1,0:T(8,128)(2,1)} copy(bf16[8,128,256]{2,1,0:T(8,128)(2,1)} %get-tuple-element.10) | data formatting | bytes 1048576
  116.4 1.6 %copy.28 = f32[128,256]{1,0:T(8,128)} copy(f32[128,256]{1,0:T(8,128)} %get-tuple-element.11) | data formatting | bytes 262144
  118.0 1.6 %copy.29 = f32[128,256]{1,0:T(8,128)} copy(f32[128,256]{1,0:T(8,128)} %get-tuple-element.12) | data formatting | bytes 262144
  119.6 1.7 %copy.30 = f32[256,256]{1,0:T(8,128)} copy(f32[256,256]{1,0:T(8,128)} %get-tuple-element.13) | data formatting | bytes 524288
  121.2 0.0 copy-done
  121.2 0.7 copy.31
Async XLA Ops:
  114.5 6.7 %copy-start = (f32[256,256]{1,0:T(8,128)S(1)}, f32[256,256]{1,0:T(8,128)}, u32[]{:S(2)}) copy-start(f32[256,256]{1,0:T(8,128)} %get-tuple-element.14) | copy-start | bytes 786436

commit v2 on v0

v2 whole, which is shorter than its diff:
```python
import heapq

import jax
import jax.numpy as jnp
from jax import lax
from jax.experimental import pallas as pl
from jax.experimental.pallas import tpu as pltpu
from jax.sharding import PartitionSpec as P

MESH = pl.DeviceIdType.MESH
F32 = jnp.float32
BF16 = jnp.bfloat16
I32 = jnp.int32
NX, NY, NZ = 4, 4, 8
CUTS = (2, 4)


def dot(a, b):
    return jnp.dot(a, b, preferred_element_type=F32)


def dot_t(a, b):
    return lax.dot_general(a, b, (((0,), (0,)), ((), ())), preferred_element_type=F32)


def sigmoid(v):
    return 0.5 + 0.5 * jnp.tanh(0.5 * v)


class Plan:
    RATE = {"sib": 2.0}
    LATENCY = {"sib": 1000}
    AHEAD = 2000

    def __init__(self):
        self.now, self.count = 0.0, 0
        self.heap, self.jobs, self.done, self.busy, self.queue = [], [], set(), {}, {}

    def later(self, time, act):
        heapq.heappush(self.heap, (time, self.count, act))
        self.count += 1

    def transfer(self, link, kib, start, act, rank=0):
        queue = self.queue.setdefault(link, [])
        heapq.heappush(queue, (rank, self.count, kib, start, act))
        self.count += 1
        if len(queue) == 1:
            self.pump(link)

    def pump(self, link):
        queue = self.queue[link]
        while queue:
            free = self.busy.get(link, 0.0) - self.AHEAD
            if free > self.now:
                self.later(free, lambda: self.pump(link))
                return
            _, _, kib, start, act = heapq.heappop(queue)
            start()
            self.now += 40
            end = max(self.now, self.busy.get(link, 0.0)) + kib * self.RATE.get(link, 22.0)
            self.busy[link] = end
            self.later(end + self.LATENCY.get(link, 1500), act)

    def job(self, needs, cost, act, gives=None):
        self.jobs.append((set(needs), cost, act, gives))

    def mark(self, flag):
        self.done.add(flag)

    def run(self):
        while self.heap or self.jobs:
            if self.heap and self.heap[0][0] <= self.now:
                self.now += 30
                heapq.heappop(self.heap)[2]()
                continue
            ready = [j for j in self.jobs if j[0] <= self.done]
            if ready:
                job = ready[0]
                self.jobs.remove(job)
                job[2]()
                self.now += job[1]
                if job[3] is not None:
                    self.done.add(job[3])
            else:
                self.now = self.heap[0][0]


def main_kernel(
    gsrc, gcnt, howner, hlocal, hcnt, features, gtiles, htiles, fstore, hstore, s1_h, n1_h, s2_h, n2_h, cot_h,
    emb, grads,
    GF, GM, GH, HF, HH, TA, TB, COT, W1, W2, W2T,
    INV, SCT, RT, PS, PR, Q, T1, FR, RB, ACC, PRE, HO, FAR, MF, GP,
    G, B1, Q1, B2, B4, FG, TBV, TBS,
    load_sem, tb_sem, sib_s, sib_r, pl_s, az_r, ax_r, bz_r, bx_r, y_s, y_r, rs_s, rs_r, ps_s, ps_r,
    a_s, a_r, b2s, b2r, b4s, b4r, b5s, b5r,
):
    grp = lax.axis_index("grp")
    wide = lax.axis_index("wide")
    z, x = wide // NX, wide % NX
    y, c = grp // 2, grp % 2
    o = 1 - c
    plan = Plan()

    def zz(d):
        return (z + d) % NZ

    def xx(d):
        return (x + d) % NX

    def yy(d):
        return (y + d) % NY

    def at(dz=0, dy=0, dx=0):
        return (yy(dy) * 2 + c, zz(dz) * NX + xx(dx))

    sib = (y * 2 + o, wide)
    STEP = {"x+": at(dx=1), "x-": at(dx=-1), "y+": at(dy=1), "y-": at(dy=-1), "z+": at(dz=1), "z-": at(dz=-1)}

    def remote(src, dst, ss, rs, dev):
        return pltpu.make_async_remote_copy(
            src_ref=src, dst_ref=dst, send_sem=ss, recv_sem=rs, device_id=dev, device_id_type=MESH
        )

    def push(link, kib, src, dst, arrives, ss, rs, then, rank):
        def arrived():
            remote(arrives, arrives, ss, rs, sib).wait_recv()
            then()

        plan.transfer(link, kib, remote(src, dst, ss, rs, STEP[link]).start, arrived, rank)

    partners = [sib]
    partners += [at(dy=dy, dx=dx) for dy in range(NY) for dx in range(NX) if (dy, dx) != (0, 0)]
    partners += [at(dz=d) for d in range(1, NZ)]
    barrier = pltpu.get_barrier_semaphore()
    for p in partners:
        pl.semaphore_signal(barrier, inc=1, device_id=p, device_id_type=MESH)

    loads = []

    def load(src, dst):
        cp = pltpu.make_async_copy(src, dst, load_sem.at[len(loads)])
        cp.start()
        loads.append(cp)
        return cp

    l_fs = load(fstore.at[c], HF.at[z, x, c])
    l_ft = load(features, GF.at[pl.ds(grp * 8, 8)])
    l_hs = load(hstore.at[c], HH.at[z, x, c])
    l_ta = load(gtiles, TA)
    l_tb = load(htiles, TB)
    l_ct = load(cot_h, COT)
    l_w = [
        load(s1_h, W1.at[pl.ds(0, 128)]), load(n1_h, W1.at[pl.ds(128, 128)]),
        load(s2_h, W2.at[pl.ds(0, 256)]), load(n2_h, W2.at[pl.ds(256, 256)]),
    ]

    lane = lax.broadcasted_iota(I32, (8, 128), 1)
    sources = [gsrc[i // 8, i % 8] for i in range(64)]
    named_row = jnp.zeros((8, 128), I32)
    for i, s in enumerate(sources):
        named_row = jnp.where(lane == i, s, named_row)
    place = jnp.zeros((8, 128), I32)
    upto = jnp.zeros((8, 128), I32)
    many = jnp.zeros((8, 128), I32)
    for i, s in enumerate(sources):
        place = place + jnp.where((s < named_row) | ((s == named_row) & (lane > i)), 1, 0)
        upto = upto + jnp.where(lane >= s, 1, 0)
        many = many + jnp.where(lane == s, 1, 0)
    place_col = jnp.transpose(jnp.broadcast_to(place[0:1], (128, 128)))[:64]
    named_col = jnp.transpose(jnp.broadcast_to(named_row[0:1], (128, 128)))[:64]
    hit = place_col == lax.broadcasted_iota(I32, (64, 128), 1)
    order = jnp.sum(jnp.where(hit, lax.broadcasted_iota(I32, (64, 128), 0), 0), axis=0, keepdims=True)
    target = jnp.sum(jnp.where(hit, named_col, 0), axis=0, keepdims=True)
    target = jnp.broadcast_to(target, (8, 128))
    same = jnp.where((target == pltpu.roll(target, 1, 1)) & (lane > 0), 1, 0)
    TBV[0:1, :] = order
    TBV[1:2, :] = order >> 3
    TBV[2:3, :] = same[0:1]
    TBV[3:4, :] = jnp.maximum(upto - 1, 0)[0:1]
    TBV[4:5, :] = jnp.minimum(many, 1)[0:1]
    l_tbl = pltpu.make_async_copy(TBV, TBS, tb_sem)
    l_tbl.start()

    class Plane:
        def __init__(self, X, n, unit, flag):
            self.X, self.n, self.unit, self.flag = X, n, unit, flag
            cut = CUTS[n]
            self.rows = {"a": (0, cut), "b": (cut, 8 - cut)}
            self.left = 16

        def at(self, zi, xi, kind, part=None):
            first, rows = self.rows[kind]
            if part is not None:
                rows = rows // 2
                first = first + part * rows
            return self.X.at[zi, xi, c, pl.ds(first, rows)]

        def kib(self, kind, part):
            return self.rows[kind][1] * self.unit / (1 if part is None else 2)

        def go(self, link, zi, xi, arrive, kind, part, rs, then):
            r = self.at(zi, xi, kind, part)
            rank = 2 * self.n + int((kind == "a") == (link[0] == "z"))
            push(link, self.kib(kind, part), r, r, self.at(*arrive, kind, part), pl_s.at[self.n], rs, then, rank)

        def share(self, zi, kind):
            first, rows = self.rows[kind]
            r = self.X.at[zi, pl.ds(0, NX), c, pl.ds(first, rows)]
            self.left -= 1
            act = self.finish if self.left == 0 else lambda: None
            copy = remote(r, r, sib_s.at[self.n], sib_r.at[self.n], sib)
            plan.transfer("sib", 4 * self.kib(kind, None), copy.start, act)

        def finish(self):
            r = self.X.at[:, :, o]
            remote(r, r, sib_s.at[self.n], sib_r.at[self.n], sib).wait()
            plan.mark(self.flag)

        def x_ring(self, kind, d, sem, have, whole):
            n, state = self.n, {"halves": 0, "units": 1}

            def unit(dx):
                have(dx)
                state["units"] += 1
                if state["units"] == 4:
                    whole()

            def half():
                state["halves"] += 1
                if state["halves"] == 2:
                    unit(2)

            def first(s):
                def then():
                    link, part = ("x+", 0) if s == 1 else ("x-", 1)
                    self.go(link, zz(d), xx(-s), (zz(d), xx(2)), kind, part, sem(2 + part), half)
                    unit(-s)

                return then

            self.go("x+", zz(d), x, (zz(d), xx(-1)), kind, None, sem(0), first(1))
            self.go("x-", zz(d), x, (zz(d), xx(1)), kind, None, sem(1), first(-1))

        def z_ring(self, kind, dx, sem, have, whole):
            state = {"halves": 0}

            def half():
                state["halves"] += 1
                if state["halves"] == 2:
                    have(4)

            def hop(s, j):
                link = "z+" if s == 1 else "z-"
                part = None if j < 4 else (0 if s == 1 else 1)

                def then():
                    if j == 4:
                        half()
                        return
                    hop(s, j + 1)
                    have(-s * j)

                index = 2 * (j - 1) + (0 if s == 1 else 1)
                self.go(link, zz(-s * (j - 1)), xx(dx), (zz(-s * j), xx(dx)), kind, part, sem(index), then)

            hop(1, 1)
            hop(-1, 1)

        def start(self):
            n = self.n
            rows_a = {}

            def have_a(dz):
                rows_a[dz % NZ] = rows_a.get(dz % NZ, 0) + 1
                if rows_a[dz % NZ] == 4:
                    self.share(zz(dz), "a")

            def a_unit(dx):
                have_a(0)
                base = 8 * (dx % NX)
                self.z_ring("a", dx, lambda i: az_r.at[n, base + i], have_a, None)

            def b_unit(dz):
                base = 4 * (dz % NZ)
                self.x_ring(
                    "b", dz, lambda i: bx_r.at[n, base + i], lambda dx: None, lambda: self.share(zz(dz), "b")
                )

            self.z_ring("b", 0, lambda i: bz_r.at[n, i], b_unit, None)
            self.x_ring("a", 0, lambda i: ax_r.at[n, i], a_unit, lambda: None)
            b_unit(0)
            a_unit(0)

    class Ring:
        def __init__(self, X, n, flag):
            self.X, self.n, self.flag, self.left = X, n, flag, 7

        def at(self, d, part):
            return self.X.at[pl.ds((yy(d) * 2 + c) * 8 + 4 * part, 4)]

        def go(self, s, d, part, index, then):
            link = "y+" if s == 1 else "y-"
            r = self.at(d, part)
            push(link, 128, r, r, self.at(d - s, part), y_s.at[self.n], y_r.at[self.n, index], then, 2 * self.n)

        def share(self, d, part=None):
            r = self.X.at[pl.ds((yy(d) * 2 + c) * 8, 8)] if part is None else self.at(d, part)
            self.left -= 1
            act = self.finish if self.left == 0 else lambda: None
            copy = remote(r, r, sib_s.at[2 + self.n], sib_r.at[2 + self.n], sib)
            plan.transfer("sib", 128, copy.start, act)

        def finish(self):
            r = self.X.at[pl.ds(0, 32)]
            remote(r, r, sib_s.at[2 + self.n], sib_r.at[2 + self.n], sib).wait()
            plan.mark(self.flag)

        def start(self):
            def lead(s, part):
                def then():
                    self.go(s, -s, part, 4 + part, lambda: self.share(2, part))
                    self.share(-s, part)

                return then

            self.go(1, 0, 0, 0, lead(1, 0))
            self.go(-1, 0, 1, 1, lead(-1, 1))
            self.go(1, 0, 1, 2, lambda: self.share(-1, 1))
            self.go(-1, 0, 0, 3, lambda: self.share(1, 0))
            self.share(0)

    def degrees(first, many):
        def act():
            @pl.loop(first, first + many)
            def _(k):
                near_live, far_live = gcnt[k], hcnt[k]
                total = jnp.zeros((128, 128), F32)
                for s in range(8):
                    t = TA[k * 8 + s].astype(F32) * jnp.where(s < near_live, 1.0, 0.0)
                    TA[k * 8 + s] = t.astype(BF16)
                    total = total + t
                for s in range(4):
                    t = TB[k * 4 + s].astype(F32) * jnp.where(s < far_live, 1.0, 0.0)
                    TB[k * 4 + s] = t.astype(BF16)
                    total = total + t
                inv = 1.0 / (1.0 + jnp.sum(total, axis=1, keepdims=True))
                INV[k] = jnp.broadcast_to(inv, (128, 128))
                SCT[k] = jnp.transpose(COT[k].astype(F32) * inv).astype(BF16)

        return act

    held = {}

    def terms(first, many):
        def term(i, acc):
            acc = acc * TBS[2, i].astype(F32) + dot(SCT[TBS[1, i]], TA[TBS[0, i]])
            RT[i] = acc.astype(BF16)
            return acc

        def act():
            start = held.get("acc")
            start = jnp.zeros((256, 128), F32) if start is None else start
            held["acc"] = lax.fori_loop(first, first + many, term, start, unroll=4)

        return act

    def partial(g):
        return RT[TBS[3, g]].astype(F32) * TBS[4, g].astype(F32)

    def for_sibling(d):
        def act():
            @pl.loop(0, 8)
            def _(i):
                PS[yy(d) * 8 + i] = partial((yy(d) * 2 + o) * 8 + i).astype(BF16)

            r = pl.ds(yy(d) * 8, 8)
            copy = remote(PS.at[r], PR.at[r], ps_s, ps_r.at[d], sib)

            def then():
                copy.wait_recv()
                plan.mark(f"PR{d}")

            plan.transfer("sib", 512, copy.start, then, -1)

        return act

    def piece(d, part):
        return Q.at[pl.ds(yy(d) * 8 + 4 * part, 4)]

    def back(link, src, dst, index, then):
        push(link, 256, src, dst, dst, rs_s, rs_r.at[index], then, 1)

    def combine(d):
        def act():
            @pl.loop(0, 8)
            def _(i):
                g = (yy(d) * 2 + c) * 8 + i
                Q[yy(d) * 8 + i] = (partial(g) + PR[yy(d) * 8 + i].astype(F32)).astype(BF16)

            if d == 2:
                back("y+", piece(2, 0), T1.at[0], 0, lambda: plan.mark("T0"))
                back("y-", piece(2, 1), T1.at[1], 1, lambda: plan.mark("T1"))
            elif d == 1:
                back("y+", piece(1, 1), FR.at[0, pl.ds(4, 4)], 2, lambda: plan.mark("R2"))
            elif d == 3:
                back("y-", piece(-1, 0), FR.at[1, pl.ds(0, 4)], 3, lambda: plan.mark("R3"))

        return act

    def onward(part):
        def act():
            d = 1 if part == 0 else -1

            @pl.loop(0, 4)
            def _(i):
                j = yy(d) * 8 + 4 * part + i
                Q[j] = (Q[j].astype(F32) + T1[part, i].astype(F32)).astype(BF16)

            link = "y+" if part == 0 else "y-"
            flag = "R4" if part == 0 else "R5"
            back(link, piece(d, part), FR.at[part, pl.ds(4 * part, 4)], 4 + part, lambda: plan.mark(flag))

        return act

    def near_one(first, many):
        def act():
            @pl.loop(first, first + many)
            def _(k):
                total = jnp.zeros((128, 128), F32)
                for s in range(8):
                    total = total + dot(TA[k * 8 + s], GF[gsrc[k, s]])
                ACC[k] = total

        return act

    def far_of(X, k, s):
        w, l = howner[s, 0, k], hlocal[s, k]
        first = (l % 2) * 4
        return jnp.concatenate([X[w // 4, w % 4, l // 2, first + i] for i in range(4)], axis=0)

    def far_one():
        for w in l_w:
            w.wait()

        @pl.loop(0, 8)
        def _(k):
            total = ACC[k]
            for s in range(4):
                total = total + dot(TB[k * 4 + s], far_of(HF, k, s))
            mean = (total * INV[k]).astype(BF16)
            GM[grp * 8 + k] = mean
            pre = dot(jnp.concatenate([GF[grp * 8 + k], mean], axis=1), W1[...])
            PRE[k] = pre
            HO[k] = (pre * sigmoid(pre)).astype(BF16)

        Ring(GM, 1, "GM").start()

    def turned():
        W2T[pl.ds(0, 256), :] = jnp.transpose(W2[pl.ds(0, 256), :].astype(F32)).astype(BF16)
        W2T[pl.ds(256, 256), :] = jnp.transpose(W2[pl.ds(256, 256), :].astype(F32)).astype(BF16)

    def scaled(total, inv):
        return jnp.concatenate([total[:, :128] * inv, total[:, 128:] * inv], axis=1).astype(BF16)

    def far_two(first, many):
        def act():
            @pl.loop(first, first + many)
            def _(k):
                total = jnp.zeros((128, 256), F32)
                for s in range(4):
                    total = total + dot(TB[k * 4 + s], far_of(HH, k, s))
                FAR[k] = total
                MF[k] = scaled(total, INV[k])

        return act

    def returned():
        @pl.loop(0, 8)
        def _(k):
            r = Q[y * 8 + k].astype(F32) + FR[0, k].astype(F32) + FR[1, k].astype(F32)
            r = jnp.transpose(r).astype(BF16)
            RB[k] = r
            total = dot(jnp.concatenate([COT[k], r], axis=1), W2T[...])
            pre = PRE[k]
            sigma = sigmoid(pre)
            GP[k] = (total * sigma * (1.0 + pre * (1.0 - sigma))).astype(BF16)

    def flat(X):
        return X[...].reshape(1024, 256)

    def put(first, rows, v):
        G[pl.ds(first, rows), :] = v[:, :128].astype(BF16)
        G[pl.ds(first + rows, rows), :] = v[:, 128:].astype(BF16)

    def gradients_one():
        own = pl.ds(grp * 8, 8)
        both = jnp.concatenate([GF[own].reshape(1024, 128), GM[own].reshape(1024, 128)], axis=1)
        v = dot_t(both, flat(GP))
        put(0, 128, v[:128])
        put(256, 128, v[128:])

    def gradient_self_two():
        put(512, 256, dot_t(flat(HO), flat(COT)))

    def gradient_neigh_two():
        put(1024, 256, dot_t(flat(HO), flat(RB)) + dot_t(flat(MF), flat(COT)))

    def wait_all(copies, flag):
        def then():
            for cp in copies:
                cp.wait_recv()
            plan.mark(flag)

        return then

    waiting = []

    def exchange(copies, cost, flag, link="all"):
        for src, dst, ss, rs, dev, arrives in copies:
            cp = remote(src, dst, ss, rs, dev)
            cp.start()
            waiting.append(cp)
        plan.now += 40 * len(copies)
        plan.later(plan.now + cost, wait_all([remote(a, a, ss, rs, dev) for _, _, ss, rs, dev, a in copies], flag))

    def reduce_sib():
        exchange([(G.at[pl.ds(o * 768, 768)], B1, a_s.at[0], a_r.at[0], sib, B1)], 1500, "B1")

    around = [(dy, dx) for dy in range(NY) for dx in range(NX) if (dy, dx) != (0, 0)]

    def reduce_xy():
        Q1[...] = (G[pl.ds(c * 768, 768), :].astype(F32) + B1[...].astype(F32)).astype(BF16)
        exchange(
            [
                (
                    Q1.at[pl.ds(yy(dy) * 192 + xx(dx) * 48, 48)], B2.at[i], b2s.at[i], b2r.at[i],
                    at(dy=dy, dx=dx), B2.at[i],
                )
                for i, (dy, dx) in enumerate(around)
            ],
            5500, "B2",
        )

    def reduce_z():
        total = Q1[pl.ds(y * 192 + x * 48, 48), :].astype(F32)
        for i in range(15):
            total = total + B2[i].astype(F32)
        B4[z] = total.astype(BF16)
        exchange(
            [
                (B4.at[z], B4.at[z], b4s.at[d - 1], b4r.at[d - 1], at(dz=d), B4.at[zz(-d)])
                for d in range(1, NZ)
            ],
            5000, "B4",
        )

    def rows(dy, dx):
        return FG.at[pl.ds(c * 768 + yy(dy) * 192 + xx(dx) * 48, 48)]

    def gather_xy():
        total = B4[0].astype(F32)
        for i in range(1, NZ):
            total = total + B4[i].astype(F32)
        FG[pl.ds(c * 768 + y * 192 + x * 48, 48), :] = total.astype(BF16)
        exchange(
            [
                (rows(0, 0), rows(0, 0), b5s.at[i], b5r.at[i], at(dy=dy, dx=dx), rows(-dy, -dx))
                for i, (dy, dx) in enumerate(around)
            ],
            5500, "B5",
        )

    def gather_sib():
        mine, other = FG.at[pl.ds(c * 768, 768)], FG.at[pl.ds(o * 768, 768)]
        exchange([(mine, mine, a_s.at[1], a_r.at[1], sib, other)], 1500, "FG")

    def group_hidden(first, many):
        def act():
            @pl.loop(first // 2, (first + many) // 2)
            def _(j):
                two = pl.ds(j * 2, 2)
                both = jnp.concatenate([GF[two].reshape(256, 128), GM[two].reshape(256, 128)], axis=1)
                pre = dot(both, W1[...])
                GH[two] = (pre * sigmoid(pre)).astype(BF16).reshape(2, 128, 256)

        return act

    def near_two(first, many):
        def act():
            @pl.loop(first, first + many)
            def _(k):
                total = FAR[k]
                for s in range(8):
                    total = total + dot(TA[k * 8 + s], GH[gsrc[k, s]])
                m = scaled(total, INV[k])
                emb[k] = dot(jnp.concatenate([HO[k], m], axis=1), W2[...]).astype(BF16)

        return act

    def start():
        l_fs.wait()
        l_ft.wait()
        pl.semaphore_wait(barrier, len(partners))
        Plane(HF, 0, 8, "HF").start()
        Ring(GF, 0, "GF").start()

        def second():
            l_hs.wait()
            Plane(HH, 1, 16, "HH").start()

        plan.later(plan.now + 300, second)

    def first_wait():
        l_ta.wait()
        l_tb.wait()
        l_ct.wait()

    start()
    plan.job(["FG"], 100, lambda: None, "end")
    plan.job(["B5"], 100, gather_sib)
    plan.job(["B4"], 200, gather_xy)
    plan.job(["B2"], 200, reduce_z)
    plan.job(["B1"], 300, reduce_xy)
    plan.job(["g1", "gs2", "gn2"], 100, reduce_sib)
    plan.job([], 50, first_wait, "in")
    plan.job(["in"], 800, degrees(0, 4), "d0")
    plan.job(["d0"], 800, degrees(4, 4), "deg")
    plan.job(["HF", "n1"], 3000, far_one, "own")
    plan.job(["deg"], 50, l_tbl.wait, "tbl")
    for i in range(4):
        plan.job([f"t{i - 1}" if i else "tbl"], 1000, terms(16 * i, 16), f"t{i}")
    for d in (2, 1, 3, 0):
        plan.job(["t3"], 150, for_sibling(d))
    for d in (2, 1, 3, 0):
        plan.job([f"PR{d}"], 300, combine(d), f"q{d}")
    plan.job(["T0", "q1"], 200, onward(0))
    plan.job(["T1", "q3"], 200, onward(1))
    plan.job(["GF", "deg"], 900, near_one(0, 4), "n0")
    plan.job(["n0"], 900, near_one(4, 4), "n1")
    plan.job(["own"], 300, turned, "W2T")
    plan.job(["R2", "R3", "R4", "R5", "q0", "W2T"], 2200, returned, "RB")
    plan.job(["RB"], 900, gradients_one, "g1")
    plan.job(["HH"], 1000, far_two(0, 4), "f0")
    plan.job(["f0"], 1000, far_two(4, 4), "f1")
    plan.job(["RB", "f1"], 1500, gradient_neigh_two, "gn2")
    plan.job(["own"], 900, gradient_self_two, "gs2")
    for i in range(8):
        plan.job([f"h{i - 1}" if i else "GM", "own"], 700, group_hidden(8 * i, 8), f"h{i}")
    for i in range(4):
        plan.job([f"e{i - 1}" if i else "h7", "f1"], 1200, near_two(2 * i, 2), f"e{i}")
    plan.run()

    grads[...] = FG[...]
    for n in range(2):
        X = (GF, GH)[n].at[pl.ds(0, 62)]
        remote(X, X, pl_s.at[n], az_r.at[n, 0], sib).wait_send()
        X = GF.at[pl.ds(0, 24)]
        remote(X, X, y_s.at[n], y_r.at[n, 0], sib).wait_send()
    X = Q.at[pl.ds(0, 24)]
    remote(X, X, rs_s, rs_r.at[0], sib).wait_send()
    remote(PS, PR, ps_s, ps_r.at[0], sib).wait_send()
    for cp in waiting:
        cp.wait_send()


def last_kernel(emb_in, grads, emb, gs1, gn1, gs2, gn2):
    emb[...] = emb_in[...]

    def take(first, rows, out):
        out[:, :128] = grads[pl.ds(first, rows), :].astype(F32)
        out[:, 128:] = grads[pl.ds(first + rows, rows), :].astype(F32)

    take(0, 128, gs1)
    take(256, 128, gn1)
    take(512, 256, gs2)
    take(1024, 256, gn2)


def body(
    features, group_src, group_count, group_tiles, hist_owner, hist_local, hist_count, hist_tiles,
    feature_store, hidden_store, self_one, neigh_one, self_two, neigh_two, cotangent,
):
    anywhere = pl.BlockSpec(memory_space=pl.ANY)
    vmem = pl.BlockSpec(memory_space=pltpu.VMEM)
    smem = pl.BlockSpec(memory_space=pltpu.SMEM)
    V, D = pltpu.VMEM, pltpu.SemaphoreType.DMA
    scratch = [
        V((64, 128, 128), BF16), V((64, 128, 128), BF16), V((64, 128, 256), BF16),
        V((8, 4, 2, 8, 32, 128), BF16), V((8, 4, 2, 8, 32, 256), BF16),
        V((64, 128, 128), BF16), V((32, 128, 128), BF16), V((8, 128, 256), BF16),
        V((256, 256), BF16), V((512, 256), BF16), V((512, 256), BF16),
        V((8, 128, 128), F32), V((8, 256, 128), BF16), V((64, 256, 128), BF16),
        V((32, 256, 128), BF16), V((32, 256, 128), BF16), V((32, 256, 128), BF16),
        V((2, 4, 256, 128), BF16), V((2, 8, 256, 128), BF16), V((8, 128, 256), BF16),
        V((8, 128, 128), F32), V((8, 128, 256), F32), V((8, 128, 256), BF16),
        V((8, 128, 256), F32), V((8, 128, 256), BF16), V((8, 128, 256), BF16),
        V((1536, 128), BF16), V((768, 128), BF16), V((768, 128), BF16),
        V((15, 48, 128), BF16), V((8, 48, 128), BF16),
        V((1536, 128), BF16), V((8, 128), I32), pltpu.SMEM((8, 128), I32),
        D((12,)), D, D((4,)), D((4,)), D((2,)),
        D((2, 32)), D((2, 4)), D((2, 8)), D((2, 32)), D((2,)), D((2, 6)), D, D((6,)), D, D((4,)),
        D((2,)), D((2,)), D((15,)), D((15,)), D((7,)), D((7,)), D((15,)), D((15,)),
    ]
    emb, grads = pl.pallas_call(
        main_kernel,
        out_shape=(jax.ShapeDtypeStruct((8, 128, 256), BF16), jax.ShapeDtypeStruct((1536, 128), BF16)),
        in_specs=[smem] * 5 + [anywhere] * 10,
        out_specs=(vmem, vmem),
        scratch_shapes=scratch,
        compiler_params=pltpu.CompilerParams(
            collective_id=0, has_side_effects=True, vmem_limit_bytes=60 * 2**20
        ),
    )(
        group_src, group_count, hist_owner.transpose(1, 2, 0), hist_local.T, hist_count,
        features, group_tiles.reshape(64, 128, 128), hist_tiles.reshape(32, 128, 128),
        feature_store.reshape(2, 8, 32, 128), hidden_store.reshape(2, 8, 32, 256),
        self_one, neigh_one, self_two, neigh_two, cotangent,
    )
    return pl.pallas_call(
        last_kernel,
        out_shape=(
            jax.ShapeDtypeStruct((8, 128, 256), BF16),
            jax.ShapeDtypeStruct((128, 256), F32),
            jax.ShapeDtypeStruct((128, 256), F32),
            jax.ShapeDtypeStruct((256, 256), F32),
            jax.ShapeDtypeStruct((256, 256), F32),
        ),
        in_specs=[vmem] * 2,
        out_specs=(vmem,) * 5,
    )(emb, grads)


def solution(mesh):
    every = P(("grp", "wide"))
    wide = P("wide")
    placed = (every,) * 8 + (wide, wide) + (P(),) * 4 + (every,)
    return jax.shard_map(
        body, mesh=mesh, in_specs=placed, out_specs=(every, P(), P(), P(), P()), check_vma=False
    )
```

time: 578 us -> 86 us (0.15)
  waiting for transfers between devices: 474 us -> 0 us
  Pallas kernels: 0 us -> 85.2 us
  local copies, waits for them, and re-layouts: 31.2 us -> 0 us
  other arithmetic: 31 us -> 0 us
  matrix products: 26.4 us -> 0 us
  between operations: 14.3 us -> 0.65 us
    psum x1 -> x0, waiting for transfers between devices: 250 us -> none  [body(): lax.psum((grad_self_one, grad_neigh_one, grad_self_two, grad_neigh_two),...]
    all_gather x4 -> x0, waiting for transfers between devices: 193 us -> none  [the longest x1 90.8 us: body(): lax.all_gather(hidden_store, 'wide', axis=0, tiled=True)]
    pallas_call x0 -> x2, Pallas kernels: none -> 85.2 us  [the longest x1 83 us: body(): pl.pallas_call(main_kernel, out_shape=(jax.ShapeDtypeStruct((8, 128, 256)...]
    reduce_scatter x1 -> x0, waiting for transfers between devices: 28.5 us -> none  [body(): lax.psum_scatter(by_target.astype(jnp.bfloat16), 'grp', scatter_dimension...]
    dot_general x14 -> x0, matrix products: 26.4 us -> none  [the longest x1 5.54 us: body(): jnp.einsum('csrj,crf->csjf', tiles_near, scaled, preferred_element_type=j...]
    scatter-add x1 -> x0, other arithmetic: 19.8 us -> none  [body(): jax.ops.segment_sum(slot_terms, sources, num_segments=group_rows)]
    gather x4 -> x0, local copies, waits for them, and re-layouts: 18 us -> none  [the longest x1 5.45 us: body(): far_hid = jnp.take(whole_hid, wanted, axis=0)]
    unnamed x33 -> x0, local copies, waits for them, and re-layouts: 7.71 us -> none
  transfers between devices with their start and end apart: 6 -> 0, of which waited for: 5 -> 0; matrix products, arithmetic and copies ran while one was open for 12% -> 0% of each run, Pallas kernels for 0% -> 0%
where the time goes in v2:
time: 86 us; the launch traced here: 85.8 us
  Pallas kernels  85.2 us (99%)
    pallas_call x1, Pallas kernels, body(): pl.pallas_call(main_kernel, out_shape=(jax.ShapeDtypeStruct((8, 128, 256)...  83 us
    pallas_call x1, Pallas kernels, body(): pl.pallas_call(last_kernel, out_shape=(jax.ShapeDtypeStruct((8, 128, 256)...  2.21 us

profile of v2, /device:TPU:1, one launch (start us, length us, event | category | flops | bytes accessed | tf_op | source)
XLA Modules:
  0.0 85.8 jit_solution(16829007390036709188)
XLA Ops:
  0.6 83.0 %shard_map.182 = (bf16[8,128,256]{2,1,0:T(8,128)(2,1)}, bf16[1536,128]{1,0:T(8,128)(2,1)}) custom-call(s32[8,8]{1,0:T(8,128)} %gsrc.1, s32[8]{0:T(128)} %gcnt.1, s32[4,1,8]{2,1,0:T(1,128)} %bitcast.10, s32[4,8]{1,0:T(4,128)} %bitcast.11, s32[8]{0:T(128)} %hcnt.1, bf16[8,128,128]{2,1,0:T(8,128)(2,1)} %features.1, bf16[64,128,128]{2,1,0:T(8,128)(2,1)} %bitcast.6, ...), custom_call_target="tpu_custom_call" | custom-call | tf_op jit(solution)/shard_map/pallas_call | solution.py:704
  83.6 2.2 %shard_map.183 = (bf16[8,128,256]{2,1,0:T(8,128)(2,1)}, f32[128,256]{1,0:T(8,128)}, f32[128,256]{1,0:T(8,128)}, f32[256,256]{1,0:T(8,128)}, f32[256,256]{1,0:T(8,128)}) custom-call(bf16[8,128,256]{2,1,0:T(8,128)(2,1)} %get-tuple-element.7.emb_in, bf16[1536,128]{1,0:T(8,128)(2,1)} %get-tuple-element.8.grads), custom_call_target="tpu_custom_call" | custom-call | tf_op jit(solution)/shard_map/pallas_call | solution.py:719

commit v3 on v2

--- a/solution.py
+++ b/solution.py
@@ -56,7 +56,7 @@
                 return
             _, _, kib, start, act = heapq.heappop(queue)
             start()
-            self.now += 40
+            self.now += 15
             end = max(self.now, self.busy.get(link, 0.0)) + kib * self.RATE.get(link, 22.0)
             self.busy[link] = end
             self.later(end + self.LATENCY.get(link, 1500), act)
@@ -70,7 +70,7 @@
     def run(self):
         while self.heap or self.jobs:
             if self.heap and self.heap[0][0] <= self.now:
-                self.now += 30
+                self.now += 15
                 heapq.heappop(self.heap)[2]()
                 continue
             ready = [j for j in self.jobs if j[0] <= self.done]
@@ -89,7 +89,7 @@
     gsrc, gcnt, howner, hlocal, hcnt, features, gtiles, htiles, fstore, hstore, s1_h, n1_h, s2_h, n2_h, cot_h,
     emb, grads,
     GF, GM, GH, HF, HH, TA, TB, COT, W1, W2, W2T,
-    INV, SCT, RT, PS, PR, Q, T1, FR, RB, ACC, PRE, HO, FAR, MF, GP,
+    INV, SCT, RT, PS, PR, Q, T1, FR, RB, ACC, PRE, FAR, MF, GP,
     G, B1, Q1, B2, B4, FG, TBV, TBS,
     load_sem, tb_sem, sib_s, sib_r, pl_s, az_r, ax_r, bz_r, bx_r, y_s, y_r, rs_s, rs_r, ps_s, ps_r,
     a_s, a_r, b2s, b2r, b4s, b4r, b5s, b5r,
@@ -154,32 +154,34 @@
         load(s2_h, W2.at[pl.ds(0, 256)]), load(n2_h, W2.at[pl.ds(256, 256)]),
     ]
 
-    lane = lax.broadcasted_iota(I32, (8, 128), 1)
-    sources = [gsrc[i // 8, i % 8] for i in range(64)]
-    named_row = jnp.zeros((8, 128), I32)
-    for i, s in enumerate(sources):
-        named_row = jnp.where(lane == i, s, named_row)
-    place = jnp.zeros((8, 128), I32)
-    upto = jnp.zeros((8, 128), I32)
-    many = jnp.zeros((8, 128), I32)
-    for i, s in enumerate(sources):
-        place = place + jnp.where((s < named_row) | ((s == named_row) & (lane > i)), 1, 0)
-        upto = upto + jnp.where(lane >= s, 1, 0)
-        many = many + jnp.where(lane == s, 1, 0)
-    place_col = jnp.transpose(jnp.broadcast_to(place[0:1], (128, 128)))[:64]
-    named_col = jnp.transpose(jnp.broadcast_to(named_row[0:1], (128, 128)))[:64]
-    hit = place_col == lax.broadcasted_iota(I32, (64, 128), 1)
-    order = jnp.sum(jnp.where(hit, lax.broadcasted_iota(I32, (64, 128), 0), 0), axis=0, keepdims=True)
-    target = jnp.sum(jnp.where(hit, named_col, 0), axis=0, keepdims=True)
-    target = jnp.broadcast_to(target, (8, 128))
-    same = jnp.where((target == pltpu.roll(target, 1, 1)) & (lane > 0), 1, 0)
-    TBV[0:1, :] = order
-    TBV[1:2, :] = order >> 3
-    TBV[2:3, :] = same[0:1]
-    TBV[3:4, :] = jnp.maximum(upto - 1, 0)[0:1]
-    TBV[4:5, :] = jnp.minimum(many, 1)[0:1]
     l_tbl = pltpu.make_async_copy(TBV, TBS, tb_sem)
-    l_tbl.start()
+
+    def slot_order():
+        lane = lax.broadcasted_iota(I32, (8, 128), 1)
+        sources = [gsrc[i // 8, i % 8] for i in range(64)]
+        named_row = jnp.zeros((8, 128), I32)
+        for i, s in enumerate(sources):
+            named_row = jnp.where(lane == i, s, named_row)
+        place = jnp.zeros((8, 128), I32)
+        upto = jnp.zeros((8, 128), I32)
+        many = jnp.zeros((8, 128), I32)
+        for i, s in enumerate(sources):
+            place = place + jnp.where((s < named_row) | ((s == named_row) & (lane > i)), 1, 0)
+            upto = upto + jnp.where(lane >= s, 1, 0)
+            many = many + jnp.where(lane == s, 1, 0)
+        place_col = jnp.transpose(jnp.broadcast_to(place[0:1], (128, 128)))[:64]
+        named_col = jnp.transpose(jnp.broadcast_to(named_row[0:1], (128, 128)))[:64]
+        hit = place_col == lax.broadcasted_iota(I32, (64, 128), 1)
+        order = jnp.sum(jnp.where(hit, lax.broadcasted_iota(I32, (64, 128), 0), 0), axis=0, keepdims=True)
+        target = jnp.sum(jnp.where(hit, named_col, 0), axis=0, keepdims=True)
+        target = jnp.broadcast_to(target, (8, 128))
+        same = jnp.where((target == pltpu.roll(target, 1, 1)) & (lane > 0), 1, 0)
+        TBV[0:1, :] = order
+        TBV[1:2, :] = order >> 3
+        TBV[2:3, :] = same[0:1]
+        TBV[3:4, :] = jnp.maximum(upto - 1, 0)[0:1]
+        TBV[4:5, :] = jnp.minimum(many, 1)[0:1]
+        l_tbl.start()
 
     class Plane:
         def __init__(self, X, n, unit, flag):
@@ -292,42 +294,59 @@
             a_unit(0)
 
     class Ring:
-        def __init__(self, X, n, flag):
-            self.X, self.n, self.flag, self.left = X, n, flag, 7
+        def __init__(self, X, n, out, kib, flag):
+            self.X, self.n, self.out, self.kib, self.flag, self.left = X, n, out, kib, flag, 8
+
+        def first(self, d, part):
+            return (yy(d) * 2 + c) * 8 + 4 * part
 
         def at(self, d, part):
-            return self.X.at[pl.ds((yy(d) * 2 + c) * 8 + 4 * part, 4)]
+            return self.X.at[pl.ds(self.first(d, part), 4)]
 
         def go(self, s, d, part, index, then):
             link = "y+" if s == 1 else "y-"
             r = self.at(d, part)
             push(link, 128, r, r, self.at(d - s, part), y_s.at[self.n], y_r.at[self.n, index], then, 2 * self.n)
 
-        def share(self, d, part=None):
-            r = self.X.at[pl.ds((yy(d) * 2 + c) * 8, 8)] if part is None else self.at(d, part)
+        def share(self, d, part):
+            r = self.out.at[pl.ds(self.first(d, part), 4)]
             self.left -= 1
             act = self.finish if self.left == 0 else lambda: None
             copy = remote(r, r, sib_s.at[2 + self.n], sib_r.at[2 + self.n], sib)
-            plan.transfer("sib", 128, copy.start, act)
+            plan.transfer("sib", self.kib, copy.start, act)
+
+        def have(self, d, part):
+            if self.out is self.X:
+                self.share(d, part)
+                return
+
+            def act():
+                @pl.loop(0, 2)
+                def _(j):
+                    two = pl.ds(self.first(d, part) + 2 * j, 2)
+                    both = jnp.concatenate([GF[two].reshape(256, 128), GM[two].reshape(256, 128)], axis=1)
+                    pre = dot(both, W1[...])
+                    GH[two] = (pre * sigmoid(pre)).astype(BF16).reshape(2, 128, 256)
+
+                self.share(d, part)
+
+            plan.job([], 400, act)
 
         def finish(self):
-            r = self.X.at[pl.ds(0, 32)]
+            r = self.out.at[pl.ds(0, 32)]
             remote(r, r, sib_s.at[2 + self.n], sib_r.at[2 + self.n], sib).wait()
             plan.mark(self.flag)
 
-        def start(self):
-            def lead(s, part):
-                def then():
-                    self.go(s, -s, part, 4 + part, lambda: self.share(2, part))
-                    self.share(-s, part)
-
-                return then
-
-            self.go(1, 0, 0, 0, lead(1, 0))
-            self.go(-1, 0, 1, 1, lead(-1, 1))
-            self.go(1, 0, 1, 2, lambda: self.share(-1, 1))
-            self.go(-1, 0, 0, 3, lambda: self.share(1, 0))
-            self.share(0)
+        def start(self, part):
+            s = 1 - 2 * part
+
+            def lead():
+                self.go(s, -s, part, 4 + part, lambda: self.have(2, part))
+                self.have(-s, part)
+
+            self.go(s, 0, part, part, lead)
+            self.go(-s, 0, part, 2 + part, lambda: self.have(s, part))
+            self.share(0, part)
 
     def degrees(first, many):
         def act():
@@ -422,38 +441,48 @@
 
         return act
 
+    def side_by_side(X, k, many):
+        return jnp.concatenate([X[k * many + s] for s in range(many)], axis=1)
+
+    def stacked(blocks):
+        return jnp.concatenate(blocks, axis=0)
+
     def near_one(first, many):
         def act():
             @pl.loop(first, first + many)
             def _(k):
-                total = jnp.zeros((128, 128), F32)
-                for s in range(8):
-                    total = total + dot(TA[k * 8 + s], GF[gsrc[k, s]])
-                ACC[k] = total
-
-        return act
-
-    def far_of(X, k, s):
-        w, l = howner[s, 0, k], hlocal[s, k]
-        first = (l % 2) * 4
-        return jnp.concatenate([X[w // 4, w % 4, l // 2, first + i] for i in range(4)], axis=0)
-
-    def far_one():
-        for w in l_w:
-            w.wait()
-
-        @pl.loop(0, 8)
-        def _(k):
-            total = ACC[k]
-            for s in range(4):
-                total = total + dot(TB[k * 4 + s], far_of(HF, k, s))
-            mean = (total * INV[k]).astype(BF16)
-            GM[grp * 8 + k] = mean
-            pre = dot(jnp.concatenate([GF[grp * 8 + k], mean], axis=1), W1[...])
-            PRE[k] = pre
-            HO[k] = (pre * sigmoid(pre)).astype(BF16)
-
-        Ring(GM, 1, "GM").start()
+                ACC[k] = dot(side_by_side(TA, k, 8), stacked([GF[gsrc[k, s]] for s in range(8)]))
+
+        return act
+
+    def far_of(X, k):
+        blocks = []
+        for s in range(4):
+            w, l = howner[s, 0, k], hlocal[s, k]
+            blocks += [X[w // 4, w % 4, l // 2, (l % 2) * 4 + i] for i in range(4)]
+        return stacked(blocks)
+
+    mean_ring = Ring(GM, 1, GH, 256, "GH")
+
+    def far_one(first, many):
+        def act():
+            if first == 0:
+                for w in l_w:
+                    w.wait()
+
+            @pl.loop(first, first + many)
+            def _(k):
+                total = ACC[k] + dot(side_by_side(TB, k, 4), far_of(HF, k))
+                mean = (total * INV[k]).astype(BF16)
+                GM[grp * 8 + k] = mean
+                pre = dot(jnp.concatenate([GF[grp * 8 + k], mean], axis=1), W1[...])
+                PRE[k] = pre
+                GH[grp * 8 + k] = (pre * sigmoid(pre)).astype(BF16)
+
+            if (first + many) % 4 == 0:
+                mean_ring.start(first // 4)
+
+        return act
 
     def turned():
         W2T[pl.ds(0, 256), :] = jnp.transpose(W2[pl.ds(0, 256), :].astype(F32)).astype(BF16)
@@ -466,24 +495,28 @@
         def act():
             @pl.loop(first, first + many)
             def _(k):
-                total = jnp.zeros((128, 256), F32)
-                for s in range(4):
-                    total = total + dot(TB[k * 4 + s], far_of(HH, k, s))
+                total = dot(side_by_side(TB, k, 4), far_of(HH, k))
                 FAR[k] = total
                 MF[k] = scaled(total, INV[k])
 
         return act
 
-    def returned():
-        @pl.loop(0, 8)
-        def _(k):
-            r = Q[y * 8 + k].astype(F32) + FR[0, k].astype(F32) + FR[1, k].astype(F32)
-            r = jnp.transpose(r).astype(BF16)
-            RB[k] = r
-            total = dot(jnp.concatenate([COT[k], r], axis=1), W2T[...])
-            pre = PRE[k]
-            sigma = sigmoid(pre)
-            GP[k] = (total * sigma * (1.0 + pre * (1.0 - sigma))).astype(BF16)
+    def returned(first, many):
+        def act():
+            @pl.loop(first, first + many)
+            def _(k):
+                r = Q[y * 8 + k].astype(F32) + FR[0, k].astype(F32) + FR[1, k].astype(F32)
+                r = jnp.transpose(r).astype(BF16)
+                RB[k] = r
+                total = dot(jnp.concatenate([COT[k], r], axis=1), W2T[...])
+                pre = PRE[k]
+                sigma = sigmoid(pre)
+                GP[k] = (total * sigma * (1.0 + pre * (1.0 - sigma))).astype(BF16)
+
+        return act
+
+    def own_hidden():
+        return GH[pl.ds(grp * 8, 8)].reshape(1024, 256)
 
     def flat(X):
         return X[...].reshape(1024, 256)
@@ -500,10 +533,13 @@
         put(256, 128, v[128:])
 
     def gradient_self_two():
-        put(512, 256, dot_t(flat(HO), flat(COT)))
+        put(512, 256, dot_t(own_hidden(), flat(COT)))
 
     def gradient_neigh_two():
-        put(1024, 256, dot_t(flat(HO), flat(RB)) + dot_t(flat(MF), flat(COT)))
+        put(1536, 256, dot_t(flat(MF), flat(COT)))
+
+    def gradient_neigh_near():
+        put(1024, 256, dot_t(own_hidden(), flat(RB)))
 
     def wait_all(copies, flag):
         def then():
@@ -523,86 +559,100 @@
         plan.now += 40 * len(copies)
         plan.later(plan.now + cost, wait_all([remote(a, a, ss, rs, dev) for _, _, ss, rs, dev, a in copies], flag))
 
-    def reduce_sib():
-        exchange([(G.at[pl.ds(o * 768, 768)], B1, a_s.at[0], a_r.at[0], sib, B1)], 1500, "B1")
-
     around = [(dy, dx) for dy in range(NY) for dx in range(NX) if (dy, dx) != (0, 0)]
 
-    def reduce_xy():
-        Q1[...] = (G[pl.ds(c * 768, 768), :].astype(F32) + B1[...].astype(F32)).astype(BF16)
-        exchange(
-            [
-                (
-                    Q1.at[pl.ds(yy(dy) * 192 + xx(dx) * 48, 48)], B2.at[i], b2s.at[i], b2r.at[i],
-                    at(dy=dy, dx=dx), B2.at[i],
-                )
-                for i, (dy, dx) in enumerate(around)
-            ],
-            5500, "B2",
-        )
-
-    def reduce_z():
-        total = Q1[pl.ds(y * 192 + x * 48, 48), :].astype(F32)
-        for i in range(15):
-            total = total + B2[i].astype(F32)
-        B4[z] = total.astype(BF16)
-        exchange(
-            [
-                (B4.at[z], B4.at[z], b4s.at[d - 1], b4r.at[d - 1], at(dz=d), B4.at[zz(-d)])
-                for d in range(1, NZ)
-            ],
-            5000, "B4",
-        )
-
-    def rows(dy, dx):
-        return FG.at[pl.ds(c * 768 + yy(dy) * 192 + xx(dx) * 48, 48)]
-
-    def gather_xy():
-        total = B4[0].astype(F32)
-        for i in range(1, NZ):
-            total = total + B4[i].astype(F32)
-        FG[pl.ds(c * 768 + y * 192 + x * 48, 48), :] = total.astype(BF16)
-        exchange(
-            [
-                (rows(0, 0), rows(0, 0), b5s.at[i], b5r.at[i], at(dy=dy, dx=dx), rows(-dy, -dx))
-                for i, (dy, dx) in enumerate(around)
-            ],
-            5500, "B5",
-        )
-
-    def gather_sib():
-        mine, other = FG.at[pl.ds(c * 768, 768)], FG.at[pl.ds(o * 768, 768)]
-        exchange([(mine, mine, a_s.at[1], a_r.at[1], sib, other)], 1500, "FG")
-
-    def group_hidden(first, many):
-        def act():
-            @pl.loop(first // 2, (first + many) // 2)
-            def _(j):
-                two = pl.ds(j * 2, 2)
-                both = jnp.concatenate([GF[two].reshape(256, 128), GM[two].reshape(256, 128)], axis=1)
-                pre = dot(both, W1[...])
-                GH[two] = (pre * sigmoid(pre)).astype(BF16).reshape(2, 128, 256)
-
-        return act
+    class Total:
+        def __init__(self, n, first, rows):
+            self.n, self.first, self.half, self.piece = n, first, rows // 2, rows // 32
+            self.some = pl.ds(n * 48, self.piece)
+
+        def rows(self, dy, dx):
+            return pl.ds(self.first + c * self.half + yy(dy) * 4 * self.piece + xx(dx) * self.piece, self.piece)
+
+        def core(self, core):
+            return pl.ds(self.first + core * self.half, self.half)
+
+        def reduce_sib(self):
+            n, r = self.n, pl.ds(self.first // 2, self.half)
+            exchange([(G.at[self.core(o)], B1.at[r], a_s.at[n, 0], a_r.at[n, 0], sib, B1.at[r])], 1100, f"B1{n}")
+
+        def reduce_xy(self):
+            n, r = self.n, self.core(c)
+            Q1[r, :] = (G[r, :].astype(F32) + B1[pl.ds(self.first // 2, self.half), :].astype(F32)).astype(BF16)
+            exchange(
+                [
+                    (
+                        Q1.at[self.rows(dy, dx)], B2.at[i, self.some], b2s.at[n, i], b2r.at[n, i],
+                        at(dy=dy, dx=dx), B2.at[i, self.some],
+                    )
+                    for i, (dy, dx) in enumerate(around)
+                ],
+                4500, f"B2{n}",
+            )
+
+        def reduce_z(self):
+            n = self.n
+            total = Q1[self.rows(0, 0), :].astype(F32)
+            for i in range(15):
+                total = total + B2[i, self.some, :].astype(F32)
+            B4[z, self.some, :] = total.astype(BF16)
+            exchange(
+                [
+                    (
+                        B4.at[z, self.some], B4.at[z, self.some], b4s.at[n, d - 1], b4r.at[n, d - 1],
+                        at(dz=d), B4.at[zz(-d), self.some],
+                    )
+                    for d in range(1, NZ)
+                ],
+                4800, f"B4{n}",
+            )
+
+        def gather_xy(self):
+            n = self.n
+            total = B4[0, self.some, :].astype(F32)
+            for i in range(1, NZ):
+                total = total + B4[i, self.some, :].astype(F32)
+            r = self.rows(0, 0)
+            FG[r, :] = total.astype(BF16)
+            exchange(
+                [
+                    (FG.at[r], FG.at[r], b5s.at[n, i], b5r.at[n, i], at(dy=dy, dx=dx), FG.at[self.rows(-dy, -dx)])
+                    for i, (dy, dx) in enumerate(around)
+                ],
+                4500, f"B5{n}",
+            )
+
+        def gather_sib(self):
+            n, mine, other = self.n, FG.at[self.core(c)], FG.at[self.core(o)]
+            exchange([(mine, mine, a_s.at[n, 1], a_r.at[n, 1], sib, other)], 1100, f"FG{n}")
+
+        def jobs(self, needs):
+            n = self.n
+            plan.job([f"B5{n}"], 50, self.gather_sib)
+            plan.job([f"B4{n}"], 100, self.gather_xy)
+            plan.job([f"B2{n}"], 100, self.reduce_z)
+            plan.job([f"B1{n}"], 150, self.reduce_xy)
+            plan.job(needs, 50, self.reduce_sib)
 
     def near_two(first, many):
         def act():
             @pl.loop(first, first + many)
             def _(k):
-                total = FAR[k]
-                for s in range(8):
-                    total = total + dot(TA[k * 8 + s], GH[gsrc[k, s]])
+                total = FAR[k] + dot(side_by_side(TA, k, 8), stacked([GH[gsrc[k, s]] for s in range(8)]))
                 m = scaled(total, INV[k])
-                emb[k] = dot(jnp.concatenate([HO[k], m], axis=1), W2[...]).astype(BF16)
+                emb[k] = dot(jnp.concatenate([GH[grp * 8 + k], m], axis=1), W2[...]).astype(BF16)
 
         return act
 
     def start():
+        slot_order()
         l_fs.wait()
         l_ft.wait()
         pl.semaphore_wait(barrier, len(partners))
         Plane(HF, 0, 8, "HF").start()
-        Ring(GF, 0, "GF").start()
+        first_ring = Ring(GF, 0, GF, 128, "GF")
+        first_ring.start(0)
+        first_ring.start(1)
 
         def second():
             l_hs.wait()
@@ -616,38 +666,35 @@
         l_ct.wait()
 
     start()
-    plan.job(["FG"], 100, lambda: None, "end")
-    plan.job(["B5"], 100, gather_sib)
-    plan.job(["B4"], 200, gather_xy)
-    plan.job(["B2"], 200, reduce_z)
-    plan.job(["B1"], 300, reduce_xy)
-    plan.job(["g1", "gs2", "gn2"], 100, reduce_sib)
+    Total(1, 1536, 512).jobs(["gn2"])
+    Total(0, 0, 1536).jobs(["g1", "gs2", "gnn"])
     plan.job([], 50, first_wait, "in")
     plan.job(["in"], 800, degrees(0, 4), "d0")
     plan.job(["d0"], 800, degrees(4, 4), "deg")
-    plan.job(["HF", "n1"], 3000, far_one, "own")
+    plan.job(["T0", "q1"], 200, onward(0))
+    plan.job(["T1", "q3"], 200, onward(1))
+    for i in range(4):
+        plan.job(["HF", f"o{i - 1}" if i else "n1"], 750, far_one(2 * i, 2), f"o{i}" if i < 3 else "own")
     plan.job(["deg"], 50, l_tbl.wait, "tbl")
-    for i in range(4):
-        plan.job([f"t{i - 1}" if i else "tbl"], 1000, terms(16 * i, 16), f"t{i}")
+    for i in range(8):
+        plan.job([f"t{i - 1}" if i else "tbl"], 500, terms(8 * i, 8), f"t{i}")
     for d in (2, 1, 3, 0):
-        plan.job(["t3"], 150, for_sibling(d))
+        plan.job(["t7"], 150, for_sibling(d))
     for d in (2, 1, 3, 0):
         plan.job([f"PR{d}"], 300, combine(d), f"q{d}")
-    plan.job(["T0", "q1"], 200, onward(0))
-    plan.job(["T1", "q3"], 200, onward(1))
     plan.job(["GF", "deg"], 900, near_one(0, 4), "n0")
     plan.job(["n0"], 900, near_one(4, 4), "n1")
     plan.job(["own"], 300, turned, "W2T")
-    plan.job(["R2", "R3", "R4", "R5", "q0", "W2T"], 2200, returned, "RB")
+    plan.job(["HH"], 800, far_two(0, 4), "f0")
+    plan.job(["f0"], 800, far_two(4, 4), "f1")
+    plan.job(["f1"], 700, gradient_neigh_two, "gn2")
+    for i in range(4):
+        plan.job(["R2", "R3", "R4", "R5", "q0", f"r{i - 1}" if i else "W2T"], 550, returned(2 * i, 2), f"r{i}" if i < 3 else "RB")
     plan.job(["RB"], 900, gradients_one, "g1")
-    plan.job(["HH"], 1000, far_two(0, 4), "f0")
-    plan.job(["f0"], 1000, far_two(4, 4), "f1")
-    plan.job(["RB", "f1"], 1500, gradient_neigh_two, "gn2")
+    plan.job(["RB"], 900, gradient_neigh_near, "gnn")
     plan.job(["own"], 900, gradient_self_two, "gs2")
-    for i in range(8):
-        plan.job([f"h{i - 1}" if i else "GM", "own"], 700, group_hidden(8 * i, 8), f"h{i}")
     for i in range(4):
-        plan.job([f"e{i - 1}" if i else "h7", "f1"], 1200, near_two(2 * i, 2), f"e{i}")
+        plan.job([f"e{i - 1}" if i else "GH", "f1"], 1000, near_two(2 * i, 2), f"e{i}")
     plan.run()
 
     grads[...] = FG[...]
@@ -674,6 +721,8 @@
     take(256, 128, gn1)
     take(512, 256, gs2)
     take(1024, 256, gn2)
+    gn2[:, :128] += grads[pl.ds(1536, 256), :].astype(F32)
+    gn2[:, 128:] += grads[pl.ds(1792, 256), :].astype(F32)
 
 
 def body(
@@ -692,18 +741,18 @@
         V((8, 128, 128), F32), V((8, 256, 128), BF16), V((64, 256, 128), BF16),
         V((32, 256, 128), BF16), V((32, 256, 128), BF16), V((32, 256, 128), BF16),
         V((2, 4, 256, 128), BF16), V((2, 8, 256, 128), BF16), V((8, 128, 256), BF16),
-        V((8, 128, 128), F32), V((8, 128, 256), F32), V((8, 128, 256), BF16),
+        V((8, 128, 128), F32), V((8, 128, 256), F32),
         V((8, 128, 256), F32), V((8, 128, 256), BF16), V((8, 128, 256), BF16),
-        V((1536, 128), BF16), V((768, 128), BF16), V((768, 128), BF16),
-        V((15, 48, 128), BF16), V((8, 48, 128), BF16),
-        V((1536, 128), BF16), V((8, 128), I32), pltpu.SMEM((8, 128), I32),
+        V((2048, 128), BF16), V((1024, 128), BF16), V((2048, 128), BF16),
+        V((15, 64, 128), BF16), V((8, 64, 128), BF16),
+        V((2048, 128), BF16), V((8, 128), I32), pltpu.SMEM((8, 128), I32),
         D((12,)), D, D((4,)), D((4,)), D((2,)),
         D((2, 32)), D((2, 4)), D((2, 8)), D((2, 32)), D((2,)), D((2, 6)), D, D((6,)), D, D((4,)),
-        D((2,)), D((2,)), D((15,)), D((15,)), D((7,)), D((7,)), D((15,)), D((15,)),
+        D((2, 2)), D((2, 2)), D((2, 15)), D((2, 15)), D((2, 7)), D((2, 7)), D((2, 15)), D((2, 15)),
     ]
     emb, grads = pl.pallas_call(
         main_kernel,
-        out_shape=(jax.ShapeDtypeStruct((8, 128, 256), BF16), jax.ShapeDtypeStruct((1536, 128), BF16)),
+        out_shape=(jax.ShapeDtypeStruct((8, 128, 256), BF16), jax.ShapeDtypeStruct((2048, 128), BF16)),
         in_specs=[smem] * 5 + [anywhere] * 10,
         out_specs=(vmem, vmem),
         scratch_shapes=scratch,

time: 86 us -> 80.7 us (0.938)
  Pallas kernels: 85.2 us -> 79.9 us
    pallas_call x1, Pallas kernels: 83 us -> 77.6 us  [body(): pl.pallas_call(main_kernel, out_shape=(jax.ShapeDtypeStruct((8, 128, 256)...]
where the time goes in v3:
time: 80.7 us; the launch traced here: 80.5 us
  Pallas kernels  79.9 us (99%)
    pallas_call x1, Pallas kernels, body(): pl.pallas_call(main_kernel, out_shape=(jax.ShapeDtypeStruct((8, 128, 256)...  77.6 us
    pallas_call x1, Pallas kernels, body(): pl.pallas_call(last_kernel, out_shape=(jax.ShapeDtypeStruct((8, 128, 256)...  2.26 us

profile of v3, /device:TPU:1, one launch (start us, length us, event | category | flops | bytes accessed | tf_op | source)
XLA Modules:
  0.0 80.5 jit_solution(2170332864526809411)
XLA Ops:
  0.6 77.6 %shard_map.182 = (bf16[8,128,256]{2,1,0:T(8,128)(2,1)}, bf16[2048,128]{1,0:T(8,128)(2,1)}) custom-call(s32[8,8]{1,0:T(8,128)} %gsrc.1, s32[8]{0:T(128)} %gcnt.1, s32[4,1,8]{2,1,0:T(1,128)} %bitcast.10, s32[4,8]{1,0:T(4,128)} %bitcast.11, s32[8]{0:T(128)} %hcnt.1, bf16[8,128,128]{2,1,0:T(8,128)(2,1)} %features.1, bf16[64,128,128]{2,1,0:T(8,128)(2,1)} %bitcast.6, ...), custom_call_target="tpu_custom_call" | custom-call | tf_op jit(solution)/shard_map/pallas_call | solution.py:753
  78.3 2.3 %shard_map.183 = (bf16[8,128,256]{2,1,0:T(8,128)(2,1)}, f32[128,256]{1,0:T(8,128)}, f32[128,256]{1,0:T(8,128)}, f32[256,256]{1,0:T(8,128)}, f32[256,256]{1,0:T(8,128)}) custom-call(bf16[8,128,256]{2,1,0:T(8,128)(2,1)} %get-tuple-element.7.emb_in, bf16[2048,128]{1,0:T(8,128)(2,1)} %get-tuple-element.8.grads), custom_call_target="tpu_custom_call" | custom-call | tf_op jit(solution)/shard_map/pallas_call | solution.py:768

commit v4 on v3

--- a/solution.py
+++ b/solution.py
@@ -87,11 +87,11 @@
 
 def main_kernel(
     gsrc, gcnt, howner, hlocal, hcnt, features, gtiles, htiles, fstore, hstore, s1_h, n1_h, s2_h, n2_h, cot_h,
-    emb, grads,
+    emb, FG,
     GF, GM, GH, HF, HH, TA, TB, COT, W1, W2, W2T,
     INV, SCT, RT, PS, PR, Q, T1, FR, RB, ACC, PRE, FAR, MF, GP,
-    G, B1, Q1, B2, B4, FG, TBV, TBS,
-    load_sem, tb_sem, sib_s, sib_r, pl_s, az_r, ax_r, bz_r, bx_r, y_s, y_r, rs_s, rs_r, ps_s, ps_r,
+    G, GN, B1, Q1, B2, B4, EB, TBV, TBS,
+    out_sem, load_sem, tb_sem, sib_s, sib_r, pl_s, az_r, ax_r, bz_r, bx_r, y_s, y_r, rs_s, rs_r, ps_s, ps_r,
     a_s, a_r, b2s, b2r, b4s, b4r, b5s, b5r,
 ):
     grp = lax.axis_index("grp")
@@ -533,38 +533,39 @@
         put(256, 128, v[128:])
 
     def gradient_self_two():
-        put(512, 256, dot_t(own_hidden(), flat(COT)))
+        put(1024, 256, dot_t(own_hidden(), flat(COT)))
 
     def gradient_neigh_two():
-        put(1536, 256, dot_t(flat(MF), flat(COT)))
+        put(512, 256, GN[...] + dot_t(flat(MF), flat(COT)))
 
     def gradient_neigh_near():
-        put(1024, 256, dot_t(own_hidden(), flat(RB)))
-
-    def wait_all(copies, flag):
+        GN[...] = dot_t(own_hidden(), flat(RB))
+
+    def exchange(copies, cost, flag):
+        sent = [remote(src, dst, ss, rs, dev) for src, dst, ss, rs, dev, _ in copies]
+        for cp in sent:
+            cp.start()
+
+        def left():
+            for cp in sent:
+                cp.wait_send()
+
         def then():
-            for cp in copies:
-                cp.wait_recv()
+            for _, _, ss, rs, dev, a in copies:
+                remote(a, a, ss, rs, dev).wait_recv()
             plan.mark(flag)
-
-        return then
-
-    waiting = []
-
-    def exchange(copies, cost, flag, link="all"):
-        for src, dst, ss, rs, dev, arrives in copies:
-            cp = remote(src, dst, ss, rs, dev)
-            cp.start()
-            waiting.append(cp)
-        plan.now += 40 * len(copies)
-        plan.later(plan.now + cost, wait_all([remote(a, a, ss, rs, dev) for _, _, ss, rs, dev, a in copies], flag))
+            plan.job([], 50, left)
+
+        plan.now += 20 * len(copies)
+        plan.later(plan.now + cost, then)
 
     around = [(dy, dx) for dy in range(NY) for dx in range(NX) if (dy, dx) != (0, 0)]
+    around.sort(key=lambda d: -min(d[0], NY - d[0]) - min(d[1], NX - d[1]))
 
     class Total:
         def __init__(self, n, first, rows):
             self.n, self.first, self.half, self.piece = n, first, rows // 2, rows // 32
-            self.some = pl.ds(n * 48, self.piece)
+            self.some = pl.ds(n * 16, self.piece)
 
         def rows(self, dy, dx):
             return pl.ds(self.first + c * self.half + yy(dy) * 4 * self.piece + xx(dx) * self.piece, self.piece)
@@ -602,7 +603,7 @@
                         B4.at[z, self.some], B4.at[z, self.some], b4s.at[n, d - 1], b4r.at[n, d - 1],
                         at(dz=d), B4.at[zz(-d), self.some],
                     )
-                    for d in range(1, NZ)
+                    for d in (4, 3, 5, 2, 6, 1, 7)
                 ],
                 4800, f"B4{n}",
             )
@@ -634,13 +635,19 @@
             plan.job([f"B1{n}"], 150, self.reduce_xy)
             plan.job(needs, 50, self.reduce_sib)
 
+    writes = []
+
     def near_two(first, many):
         def act():
             @pl.loop(first, first + many)
             def _(k):
                 total = FAR[k] + dot(side_by_side(TA, k, 8), stacked([GH[gsrc[k, s]] for s in range(8)]))
                 m = scaled(total, INV[k])
-                emb[k] = dot(jnp.concatenate([GH[grp * 8 + k], m], axis=1), W2[...]).astype(BF16)
+                EB[k] = dot(jnp.concatenate([GH[grp * 8 + k], m], axis=1), W2[...]).astype(BF16)
+
+            cp = pltpu.make_async_copy(EB.at[pl.ds(first, many)], emb.at[pl.ds(first, many)], out_sem.at[first])
+            cp.start()
+            writes.append(cp)
 
         return act
 
@@ -666,8 +673,8 @@
         l_ct.wait()
 
     start()
-    Total(1, 1536, 512).jobs(["gn2"])
-    Total(0, 0, 1536).jobs(["g1", "gs2", "gnn"])
+    Total(1, 0, 1024).jobs(["g1", "gn2"])
+    Total(0, 1024, 512).jobs(["gs2"])
     plan.job([], 50, first_wait, "in")
     plan.job(["in"], 800, degrees(0, 4), "d0")
     plan.job(["d0"], 800, degrees(4, 4), "deg")
@@ -684,20 +691,21 @@
         plan.job([f"PR{d}"], 300, combine(d), f"q{d}")
     plan.job(["GF", "deg"], 900, near_one(0, 4), "n0")
     plan.job(["n0"], 900, near_one(4, 4), "n1")
+    plan.job(["own"], 900, gradient_self_two, "gs2")
     plan.job(["own"], 300, turned, "W2T")
     plan.job(["HH"], 800, far_two(0, 4), "f0")
     plan.job(["f0"], 800, far_two(4, 4), "f1")
-    plan.job(["f1"], 700, gradient_neigh_two, "gn2")
     for i in range(4):
         plan.job(["R2", "R3", "R4", "R5", "q0", f"r{i - 1}" if i else "W2T"], 550, returned(2 * i, 2), f"r{i}" if i < 3 else "RB")
     plan.job(["RB"], 900, gradients_one, "g1")
     plan.job(["RB"], 900, gradient_neigh_near, "gnn")
-    plan.job(["own"], 900, gradient_self_two, "gs2")
-    for i in range(4):
-        plan.job([f"e{i - 1}" if i else "GH", "f1"], 1000, near_two(2 * i, 2), f"e{i}")
+    plan.job(["gnn", "f1"], 900, gradient_neigh_two, "gn2")
+    for i in range(8):
+        plan.job([f"e{i - 1}" if i else "GH", "f1"], 500, near_two(i, 1), f"e{i}")
     plan.run()
 
-    grads[...] = FG[...]
+    for cp in writes:
+        cp.wait()
     for n in range(2):
         X = (GF, GH)[n].at[pl.ds(0, 62)]
         remote(X, X, pl_s.at[n], az_r.at[n, 0], sib).wait_send()
@@ -706,8 +714,6 @@
     X = Q.at[pl.ds(0, 24)]
     remote(X, X, rs_s, rs_r.at[0], sib).wait_send()
     remote(PS, PR, ps_s, ps_r.at[0], sib).wait_send()
-    for cp in waiting:
-        cp.wait_send()
 
 
 def last_kernel(emb_in, grads, emb, gs1, gn1, gs2, gn2):
@@ -719,10 +725,8 @@
 
     take(0, 128, gs1)
     take(256, 128, gn1)
-    take(512, 256, gs2)
-    take(1024, 256, gn2)
-    gn2[:, :128] += grads[pl.ds(1536, 256), :].astype(F32)
-    gn2[:, 128:] += grads[pl.ds(1792, 256), :].astype(F32)
+    take(512, 256, gn2)
+    take(1024, 256, gs2)
 
 
 def body(
@@ -743,18 +747,18 @@
         V((2, 4, 256, 128), BF16), V((2, 8, 256, 128), BF16), V((8, 128, 256), BF16),
         V((8, 128, 128), F32), V((8, 128, 256), F32),
         V((8, 128, 256), F32), V((8, 128, 256), BF16), V((8, 128, 256), BF16),
-        V((2048, 128), BF16), V((1024, 128), BF16), V((2048, 128), BF16),
-        V((15, 64, 128), BF16), V((8, 64, 128), BF16),
-        V((2048, 128), BF16), V((8, 128), I32), pltpu.SMEM((8, 128), I32),
-        D((12,)), D, D((4,)), D((4,)), D((2,)),
+        V((1536, 128), BF16), V((256, 256), F32), V((768, 128), BF16), V((1536, 128), BF16),
+        V((15, 48, 128), BF16), V((8, 48, 128), BF16),
+        V((8, 128, 256), BF16), V((8, 128), I32), pltpu.SMEM((8, 128), I32),
+        D((8,)), D((12,)), D, D((4,)), D((4,)), D((2,)),
         D((2, 32)), D((2, 4)), D((2, 8)), D((2, 32)), D((2,)), D((2, 6)), D, D((6,)), D, D((4,)),
         D((2, 2)), D((2, 2)), D((2, 15)), D((2, 15)), D((2, 7)), D((2, 7)), D((2, 15)), D((2, 15)),
     ]
     emb, grads = pl.pallas_call(
         main_kernel,
-        out_shape=(jax.ShapeDtypeStruct((8, 128, 256), BF16), jax.ShapeDtypeStruct((2048, 128), BF16)),
+        out_shape=(jax.ShapeDtypeStruct((8, 128, 256), BF16), jax.ShapeDtypeStruct((1536, 128), BF16)),
         in_specs=[smem] * 5 + [anywhere] * 10,
-        out_specs=(vmem, vmem),
+        out_specs=(anywhere, vmem),
         scratch_shapes=scratch,
         compiler_params=pltpu.CompilerParams(
             collective_id=0, has_side_effects=True, vmem_limit_bytes=60 * 2**20

time: 80.7 us -> 79.8 us (0.989)
  Pallas kernels: 79.9 us -> 79 us
    pallas_call x1, Pallas kernels: 77.6 us -> 76.8 us  [body(): pl.pallas_call(main_kernel, out_shape=(jax.ShapeDtypeStruct((8, 128, 256)...]
where the time goes in v4:
time: 79.8 us; the launch traced here: 79.6 us
  Pallas kernels  79 us (99%)
    pallas_call x1, Pallas kernels, body(): pl.pallas_call(main_kernel, out_shape=(jax.ShapeDtypeStruct((8, 128, 256)...  76.8 us
    pallas_call x1, Pallas kernels, body(): pl.pallas_call(last_kernel, out_shape=(jax.ShapeDtypeStruct((8, 128, 256)...  2.21 us

profile of v4, /device:TPU:1, one launch (start us, length us, event | category | flops | bytes accessed | tf_op | source)
XLA Modules:
  0.0 79.6 jit_solution(11327870876273615048)
XLA Ops:
  0.6 76.8 %shard_map.182 = (bf16[8,128,256]{2,1,0:T(8,128)(2,1)}, bf16[1536,128]{1,0:T(8,128)(2,1)}) custom-call(s32[8,8]{1,0:T(8,128)} %gsrc.1, s32[8]{0:T(128)} %gcnt.1, s32[4,1,8]{2,1,0:T(1,128)} %bitcast.10, s32[4,8]{1,0:T(4,128)} %bitcast.11, s32[8]{0:T(128)} %hcnt.1, bf16[8,128,128]{2,1,0:T(8,128)(2,1)} %features.1, bf16[64,128,128]{2,1,0:T(8,128)(2,1)} %bitcast.6, ...), custom_call_target="tpu_custom_call" | custom-call | tf_op jit(solution)/shard_map/pallas_call | solution.py:757
  77.4 2.2 %shard_map.183 = (bf16[8,128,256]{2,1,0:T(8,128)(2,1)}, f32[128,256]{1,0:T(8,128)}, f32[128,256]{1,0:T(8,128)}, f32[256,256]{1,0:T(8,128)}, f32[256,256]{1,0:T(8,128)}) custom-call(bf16[8,128,256]{2,1,0:T(8,128)(2,1)} %get-tuple-element.7.emb_in, bf16[1536,128]{1,0:T(8,128)(2,1)} %get-tuple-element.8.grads), custom_call_target="tpu_custom_call" | custom-call | tf_op jit(solution)/shard_map/pallas_call | solution.py:772
